TPU v7x, 512 devices: a whole 4x4x16 slice. The times are simulated.
512 devices in a mesh: slab: 256 (over y, x, z), col: 2 (over core).
Axes of the slice: x: 4, y: 4, z: 16, core: 2. Of those that a mesh axis runs over, the one named last changes fastest.
Arguments:
- displacement: float32 [3, 1024, 128, 256], P(None, 'slab', 'col'), may hold values from -6 to 6
- velocity: float32 [3, 1024, 128, 256], P(None, 'slab', 'col'), may hold values from -6 to 6
- damage: float32 [1024, 128, 256], P('slab', 'col'), may hold values from 0.5 to 1.5
- broken: int32 [2, 1024, 128, 256], P(None, 'slab', 'col'), may hold values from 0 to 255, as said below
- counts: int32 [256, 4], replicated, may hold values from 0 to 64, as said below
- bits: int32 [4], replicated, may hold values from 0 to 3, each once
Outputs:
- relocated: float32 [6, 1024, 128, 256], P(None, 'slab', 'col')
Inputs may be any that keep to these rules, and one draw needn't show every extreme that they name: Each bit of a plane of broken marks one forward bond as broken. `counts`: in every aligned group of 16 slabs, the slabs at offsets 0, 1, 2, 4 and 8 of the group offer 64 columns in every round. `bits`: each bit 0..3 is used in exactly one round.
All inputs are finite; a program needn't handle non-finite values.
Results may differ from a plain program's by a relative error of at most 0.00002.
Values sent between devices are 32-bit elements; how exact they have to be, the bound alone decides.
No kernel may reach another device: no remote copies, remote signals or barrier semaphores. Data moves between devices by JAX's collectives and lax.ppermute only.
A program may use at most 64 MiB of HBM per device.

v0:
```python
import functools
import math

import jax
import jax.numpy as jnp
from jax import lax
from jax.sharding import PartitionSpec as P


def from_partner(block, axis, bit):
    count = lax.axis_size(axis)
    route = []
    for low in range(count):
        high = low | 1 << bit
        if high != low and high < count:
            route += [(low, high), (high, low)]
    return lax.ppermute(block, axis, route)


def shifted(block, axis, distance):
    devices = range(lax.axis_size(axis))
    route = [(i - distance, i) for i in devices if i - distance in devices]
    return lax.ppermute(block, axis, route)


def padded(block, sides, width):
    for axis, dim in sides:
        count = lax.axis_size(axis)
        forward = [(i, i + 1) for i in range(count - 1)]
        backward = [(target, source) for source, target in forward]
        low = lax.ppermute(
            lax.slice_in_dim(block, block.shape[dim] - width, None, axis=dim), axis, forward
        )
        high = lax.ppermute(lax.slice_in_dim(block, 0, width, axis=dim), axis, backward)
        block = jnp.concatenate([low, block, high], axis=dim)
    return block


def bond_table():
    table = []
    for step_x in range(-2, 3):
        for step_y in range(-2, 3):
            for step_z in range(-2, 3):
                square = step_x * step_x + step_y * step_y + step_z * step_z
                if 0 < square <= 4 and (step_x, step_y, step_z) > (0, 0, 0):
                    length = math.sqrt(square)
                    table.append((step_x, step_y, step_z, (1.0 - length / 2.5) / length**3))
    return table


def bond_term(own_part, other_part, step_x, step_y, step_z, weight, source, bit_index):
    alive = 1.0 - jnp.bitwise_and(jnp.right_shift(source, bit_index), 1).astype(jnp.float32)
    along = (
        step_x * (other_part[0] - own_part[0])
        + step_y * (other_part[1] - own_part[1])
        + step_z * (other_part[2] - own_part[2])
    )
    factor = weight * own_part[3] * other_part[3] * alive * along
    return jnp.stack([factor * step_x, factor * step_y, factor * step_z])


def swap_columns(head, bit_number):
    return from_partner(head, "slab", bit_number)


def on_device(displacement, velocity, damage, broken, counts, bits):
    planes, rows, cells = damage.shape
    fields = jnp.concatenate([displacement, damage[None]], 0)
    forward_data = shifted(fields[:, :2], "slab", -1)
    extended = jnp.concatenate([fields, forward_data], 1)
    extended = padded(extended, (("col", 2),), 2)
    extended = jnp.pad(extended, ((0, 0), (0, 0), (0, 0), (2, 2)))
    own_part = extended[:, 0:planes, 2 : rows + 2, 2 : cells + 2]
    own_force = jnp.zeros((3, planes, rows, cells), jnp.float32)
    reaction = jnp.zeros((3, planes + 2, rows + 4, cells), jnp.float32)
    for index, (step_x, step_y, step_z, weight) in enumerate(bond_table()):
        other_part = extended[
            :,
            step_x : step_x + planes,
            2 + step_y : 2 + step_y + rows,
            2 + step_z : 2 + step_z + cells,
        ]
        term = bond_term(
            own_part, other_part, step_x, step_y, step_z, weight, broken[index // 8], index % 8
        )
        own_force = own_force + term
        placed = lax.pad(
            -term,
            jnp.float32(0.0),
            ((0, 0, 0), (step_x, 2 - step_x, 0), (2 + step_y, 2 - step_y, 0), (step_z, -step_z, 0)),
        )
        reaction = reaction + placed
    position = lax.axis_index("col")
    lower_rim = reaction[:, :, 0:2]
    upper_rim = reaction[:, :, rows + 2 : rows + 4]
    outgoing = jnp.where(position == 0, upper_rim, lower_rim)
    incoming = from_partner(outgoing, "col", 0)
    middle = reaction[:, :, 2 : rows + 2]
    middle = middle.at[:, :, rows - 2 : rows].add(jnp.where(position == 0, incoming, 0.0))
    middle = middle.at[:, :, 0:2].add(jnp.where(position == 1, incoming, 0.0))
    ghost_part = middle[:, planes : planes + 2]
    returned = shifted(ghost_part, "slab", 1)
    force = middle[:, :planes] + own_force
    force = force.at[:, 0:2].add(returned)
    new_velocity = velocity + 0.1 * force
    new_displacement = displacement + 0.1 * new_velocity
    state = jnp.concatenate([new_displacement, new_velocity], 0)
    columns = state.reshape(6, planes * rows, cells)
    capacity = planes * rows // 4
    position = lax.axis_index("slab")
    branches = [
        functools.partial(swap_columns, bit_number=number) for number in range(bits.shape[0])
    ]
    column_index = jnp.arange(capacity, dtype=jnp.int32)
    for round_index in range(bits.shape[0]):
        partner = jnp.bitwise_xor(position, jnp.left_shift(jnp.int32(1), bits[round_index]))
        taken = jnp.minimum(counts[position, round_index], counts[partner, round_index])
        leading = columns[:, :capacity]
        received = lax.switch(bits[round_index], branches, leading)
        leading = jnp.where((column_index < taken)[None, :, None], received, leading)
        columns = columns.at[:, :capacity].set(leading)
    return columns.reshape(6, planes, rows, cells)


def solution(mesh):
    return jax.shard_map(
        on_device,
        mesh=mesh,
        in_specs=(
            P(None, "slab", "col", None),
            P(None, "slab", "col", None),
            P("slab", "col", None),
            P(None, "slab", "col", None),
            P(),
            P(),
        ),
        out_specs=P(None, "slab", "col", None),
        check_vma=False,
    )
```

profile of v0, /device:TPU:24, one launch (start us, length us, event | category | flops | bytes accessed | tf_op | source)
XLA Modules:
  0.0 181.0 jit_solution(13068161622435396586)
XLA Ops:
  0.0 1.2 pad_maximum_fusion.18
  1.2 13.8 %collective-permute-start.16 = (f32[4,2,64,256]{3,2,1,0:T(8,128)S(1)}, f32[4,2,64,256]{3,2,1,0:T(8,128)S(1)}, u32[]{:S(2)}, u32[]{:S(2)}) collective-permute-start(f32[4,2,64,256]{3,2,1,0:T(8,128)S(1)} %pad_maximum_fusion.18), channel_id=1, source_target_pairs={{2,0},{4,2},{6,4},{8,6},{10,8},{12,10},{14,12},{16,14},{18,16},{20... | collective-permute-start | bytes 1572872 | tf_op jit(solution)/shard_map/ppermute | solution.py:23
  23.7 2.5 %collective-permute-done.16 = f32[4,2,64,256]{3,2,1,0:T(8,128)S(1)} collective-permute-done((f32[4,2,64,256]{3,2,1,0:T(8,128)S(1)}, f32[4,2,64,256]{3,2,1,0:T(8,128)S(1)}, u32[]{:S(2)}, u32[]{:S(2)}) %collective-permute-start.16) | collective-permute-done | bytes 524320 | tf_op jit(solution)/shard_map/ppermute | solution.py:23
  26.2 1.3 collective-permute-start.17
  27.5 1.4 collective-permute-start.18
  30.1 0.7 collective-permute-done.18
  31.4 1.0 select_maximum_fusion
  33.0 1.1 fusion.127
  34.0 0.7 broadcast_multiply_fusion.11
  37.2 1.0 pad_slice_fusion.9
  39.7 5.5 %fusion.15 = f32[3,6,68,256]{3,2,1,0:T(8,128)S(1)} fusion(f32[3,4,64,256]{3,2,1,0:T(8,128)S(1)} %get-tuple-element.192, f32[3,4,64,256]{3,2,1,0:T(8,128)S(1)} %get-tuple-element.193, f32[3,4,64,256]{3,2,1,0:T(8,128)S(1)} %get-tuple-element.194, f32[3,4,64,256]{3,2,1,0:T(8,128)S(1)} %get-tuple-element.196, f32[3,4,64,256]{3,2,1,0:T(8,128)S(1)} %get-tuple-element.198, ...), kind=kLoop, calls=%fused_computation.33 | loop fusion | flops 4700160 | bytes 13467648 | tf_op jit(solution)/shard_map/add | solution.py:92
  45.2 2.4 %collective-permute-start.19 = (f32[3,6,2,256]{3,2,1,0:T(2,128)S(1)}, f32[3,6,2,256]{3,2,1,0:T(2,128)S(1)}, u32[]{:S(2)}, u32[]{:S(2)}) collective-permute-start(f32[3,6,2,256]{3,2,1,0:T(2,128)S(1)} %slice_select_fusion), channel_id=1, source_target_pairs={{0,1},{1,0},{2,3},{3,2},{4,5},{5,4},{6,7},{7,6},{8,9},{9,8},{10,11... | collective-permute-start | bytes 110600 | tf_op jit(solution)/shard_map/ppermute | solution.py:17
  50.5 2.1 %collective-permute-start.20 = (f32[3,2,64,256]{3,2,1,0:T(8,128)S(1)}, f32[3,2,64,256]{3,2,1,0:T(8,128)S(1)}, u32[]{:S(2)}, u32[]{:S(2)}) collective-permute-start(f32[3,2,64,256]{3,2,1,0:T(8,128)S(1)} %slice.812), channel_id=1, source_target_pairs={{0,2},{2,4},{4,6},{6,8},{8,10},{10,12},{12,14},{14,16},{16,18},{18... | collective-permute-start | bytes 1179656 | tf_op jit(solution)/shard_map/ppermute | solution.py:23
  52.7 3.5 %slice_add_fusion = f32[3,4,64,256]{3,2,1,0:T(8,128)S(1)} fusion(f32[3,6,64,256]{3,2,1,0:T(8,128)S(1)} %fusion.125, f32[1,4,64,256]{3,2,1,0:T(8,128)} %copy-done.32, f32[1,4,64,256]{3,2,1,0:T(8,128)S(1)} %copy-done.5, f32[1,4,64,256]{3,2,1,0:T(8,128)S(1)} %copy-done.13, f32[1,4,64,256]{3,2,1,0:T(8,128)S(1)} %copy-done.15, f32[1,4,64,256]{3,2,1,0:T(8,128)} %copy-done.28, ...), kind=kLoop, calls=%fused_computation.34 | loop fusion | flops 9043968 | bytes 10485760 | tf_op jit(solution)/shard_map/add | solution.py:103
  56.2 12.3 %collective-permute-done.20 = f32[3,2,64,256]{3,2,1,0:T(8,128)S(1)} collective-permute-done((f32[3,2,64,256]{3,2,1,0:T(8,128)S(1)}, f32[3,2,64,256]{3,2,1,0:T(8,128)S(1)}, u32[]{:S(2)}, u32[]{:S(2)}) %collective-permute-start.20) | collective-permute-done | bytes 393248 | tf_op jit(solution)/shard_map/ppermute | solution.py:23
  69.0 16.6 %conditional.4 = (f32[6,64,256]{2,1,0:T(8,128)}) conditional(s32[]{:T(128)} %bitcast.11, f32[6,64,256]{2,1,0:T(8,128)S(1)} %slice.813, f32[6,64,256]{2,1,0:T(8,128)S(1)} %slice.813, f32[6,64,256]{2,1,0:T(8,128)S(1)} %slice.813, f32[6,64,256]{2,1,0:T(8,128)S(1)} %slice.813), branch_computations={%region_0.1_spmd, %region_1.2_spmd, %region_2.3_spmd, %region_3.4_... | conditional | bytes 1572912 | solution.py:119
  69.0 1.9 %collective-permute-start.1 = (f32[6,64,256]{2,1,0:T(8,128)S(1)}, f32[6,64,256]{2,1,0:T(8,128)}, u32[]{:S(2)}, u32[]{:S(2)}) collective-permute-start(f32[6,64,256]{2,1,0:T(8,128)S(1)} %param.15), channel_id=1, source_target_pairs={{0,4},{4,0},{2,6},{6,2},{8,12},{12,8},{10,14},{14,10},{16,20},{20,... | collective-permute-start | bytes 1179656 | tf_op jit(solution)/shard_map/cond/branch_1_fun/ppermute | solution.py:17
  70.9 14.7 %collective-permute-done.1 = f32[6,64,256]{2,1,0:T(8,128)} collective-permute-done((f32[6,64,256]{2,1,0:T(8,128)S(1)}, f32[6,64,256]{2,1,0:T(8,128)}, u32[]{:S(2)}, u32[]{:S(2)}) %collective-permute-start.1) | collective-permute-done | bytes 393248 | tf_op jit(solution)/shard_map/cond/branch_1_fun/ppermute | solution.py:17
  85.6 1.1 broadcast_select_fusion.2
  86.7 13.1 %conditional.5 = (f32[6,64,256]{2,1,0:T(8,128)}) conditional(s32[]{:T(128)} %bitcast.14, f32[6,64,256]{2,1,0:T(8,128)S(1)} %broadcast_select_fusion.2, f32[6,64,256]{2,1,0:T(8,128)S(1)} %broadcast_select_fusion.2, f32[6,64,256]{2,1,0:T(8,128)S(1)} %broadcast_select_fusion.2, ...), branch_computations={%region_4.5_spmd, %region_5.6_spmd, %region_6.7_spmd, %region_7.8_... | conditional | bytes 1572912 | solution.py:119
  86.8 1.9 %collective-permute-start.4 = (f32[6,64,256]{2,1,0:T(8,128)S(1)}, f32[6,64,256]{2,1,0:T(8,128)}, u32[]{:S(2)}, u32[]{:S(2)}) collective-permute-start(f32[6,64,256]{2,1,0:T(8,128)S(1)} %param.18), channel_id=1, source_target_pairs={{0,2},{2,0},{4,6},{6,4},{8,10},{10,8},{12,14},{14,12},{16,18},{18,... | collective-permute-start | bytes 1179656 | tf_op jit(solution)/shard_map/cond/branch_0_fun/ppermute | solution.py:17
  88.7 11.1 %collective-permute-done.4 = f32[6,64,256]{2,1,0:T(8,128)} collective-permute-done((f32[6,64,256]{2,1,0:T(8,128)S(1)}, f32[6,64,256]{2,1,0:T(8,128)}, u32[]{:S(2)}, u32[]{:S(2)}) %collective-permute-start.4) | collective-permute-done | bytes 393248 | tf_op jit(solution)/shard_map/cond/branch_0_fun/ppermute | solution.py:17
  99.8 1.1 constant_dynamic-update-slice_fusion.1
  100.9 46.1 %conditional.6 = (f32[6,64,256]{2,1,0:T(8,128)}) conditional(s32[]{:T(128)} %bitcast.17, f32[6,64,256]{2,1,0:T(8,128)S(1)} %get-tuple-element.128, f32[6,64,256]{2,1,0:T(8,128)S(1)} %get-tuple-element.128, f32[6,64,256]{2,1,0:T(8,128)S(1)} %get-tuple-element.128, f32[6,64,256]{2,1,0:T(8,128)S(1)} %get-tuple-element.128), branch_computations={%region_8.9_spmd, %region_9.10_spmd, %region_10.11_spmd, %region_1... | conditional | bytes 1572912 | solution.py:119
  100.9 6.8 %collective-permute-start.11 = (f32[6,64,256]{2,1,0:T(8,128)S(1)}, f32[6,64,256]{2,1,0:T(8,128)}, u32[]{:S(2)}, u32[]{:S(2)}) collective-permute-start(f32[6,64,256]{2,1,0:T(8,128)S(1)} %param.25), channel_id=1, source_target_pairs={{0,16},{16,0},{2,18},{18,2},{4,20},{20,4},{6,22},{22,6},{8,24},{24... | collective-permute-start | bytes 1179656 | tf_op jit(solution)/shard_map/cond/branch_3_fun/ppermute | solution.py:17
  107.7 39.3 %collective-permute-done.11 = f32[6,64,256]{2,1,0:T(8,128)} collective-permute-done((f32[6,64,256]{2,1,0:T(8,128)S(1)}, f32[6,64,256]{2,1,0:T(8,128)}, u32[]{:S(2)}, u32[]{:S(2)}) %collective-permute-start.11) | collective-permute-done | bytes 393248 | tf_op jit(solution)/shard_map/cond/branch_3_fun/ppermute | solution.py:17
  147.1 1.1 constant_dynamic-update-slice_fusion
  148.2 30.5 %conditional.7 = (f32[6,64,256]{2,1,0:T(8,128)}) conditional(s32[]{:T(128)} %bitcast.20, f32[6,64,256]{2,1,0:T(8,128)S(1)} %get-tuple-element.126, f32[6,64,256]{2,1,0:T(8,128)S(1)} %get-tuple-element.126, f32[6,64,256]{2,1,0:T(8,128)S(1)} %get-tuple-element.126, f32[6,64,256]{2,1,0:T(8,128)S(1)} %get-tuple-element.126), branch_computations={%region_12.13_spmd, %region_13.14_spmd, %region_14.15_spmd, %regio... | conditional | bytes 1572912 | solution.py:119
  148.2 1.9 %collective-permute-start.14 = (f32[6,64,256]{2,1,0:T(8,128)S(1)}, f32[6,64,256]{2,1,0:T(8,128)}, u32[]{:S(2)}, u32[]{:S(2)}) collective-permute-start(f32[6,64,256]{2,1,0:T(8,128)S(1)} %param.28), channel_id=1, source_target_pairs={{0,8},{8,0},{2,10},{10,2},{4,12},{12,4},{6,14},{14,6},{16,24},{24,... | collective-permute-start | bytes 1179656 | tf_op jit(solution)/shard_map/cond/branch_2_fun/ppermute | solution.py:17
  150.1 28.6 %collective-permute-done.14 = f32[6,64,256]{2,1,0:T(8,128)} collective-permute-done((f32[6,64,256]{2,1,0:T(8,128)S(1)}, f32[6,64,256]{2,1,0:T(8,128)}, u32[]{:S(2)}, u32[]{:S(2)}) %collective-permute-start.14) | collective-permute-done | bytes 393248 | tf_op jit(solution)/shard_map/cond/branch_2_fun/ppermute | solution.py:17
  178.7 1.1 select_dynamic-update-slice_fusion
  179.8 1.1 copy-done.3
  (135 shorter events, 8.0 us)
Async XLA Ops:
  0.0 26.2 %copy-start = (f32[3,4,64,256]{3,2,1,0:T(8,128)S(1)}, f32[3,4,64,256]{3,2,1,0:T(8,128)}, u32[]{:S(2)}) copy-start(f32[3,4,64,256]{3,2,1,0:T(8,128)} %param.36) | copy-start | bytes 2359300
  0.0 26.2 %copy-start.1 = (f32[4,64,256]{2,1,0:T(8,128)S(1)}, f32[4,64,256]{2,1,0:T(8,128)}, u32[]{:S(2)}) copy-start(f32[4,64,256]{2,1,0:T(8,128)} %param.38) | copy-start | bytes 786436
  0.0 15.0 %copy-start.45 = (s32[4]{0:T(128)S(1)}, s32[4]{0:T(128)}, u32[]{:S(2)}) copy-start(s32[4]{0:T(128)} %param.41) | copy-start | bytes 52
  0.0 18.1 %copy-start.46 = (s32[256,4]{0,1:T(4,128)S(1)}, s32[256,4]{0,1:T(4,128)}, u32[]{:S(2)}) copy-start(s32[256,4]{0,1:T(4,128)} %param.40) | copy-start | bytes 12292
  1.2 24.9 %collective-permute-start.16 = (f32[4,2,64,256]{3,2,1,0:T(8,128)S(1)}, f32[4,2,64,256]{3,2,1,0:T(8,128)S(1)}, u32[]{:S(2)}, u32[]{:S(2)}) collective-permute-start(f32[4,2,64,256]{3,2,1,0:T(8,128)S(1)} %pad_maximum_fusion.18), channel_id=1, source_target_pairs={{2,0},{4,2},{6,4},{8,6},{10,8},{12,10},{14,12},{16,14},{18,16},{20... | collective-permute-start | bytes 1572872 | tf_op jit(solution)/shard_map/ppermute | solution.py:23
  26.2 5.2 %collective-permute-start.17 = (f32[4,6,2,256]{3,2,1,0:T(2,128)S(1)}, f32[4,6,2,256]{3,2,1,0:T(2,128)S(1)}, u32[]{:S(2)}, u32[]{:S(2)}) collective-permute-start(f32[4,6,2,256]{3,2,1,0:T(2,128)S(1)} %get-tuple-element.177), channel_id=1, source_target_pairs={{0,1},{2,3},{4,5},{6,7},{8,9},{10,11},{12,13},{14,15},{16,17},{18,... | collective-permute-start | bytes 147464 | tf_op jit(solution)/shard_map/ppermute | solution.py:31
  27.5 3.3 %collective-permute-start.18 = (f32[4,6,2,256]{3,2,1,0:T(2,128)S(1)}, f32[4,6,2,256]{3,2,1,0:T(2,128)S(1)}, u32[]{:S(2)}, u32[]{:S(2)}) collective-permute-start(f32[4,6,2,256]{3,2,1,0:T(2,128)S(1)} %get-tuple-element.178), channel_id=1, source_target_pairs={{1,0},{3,2},{5,4},{7,6},{9,8},{11,10},{13,12},{15,14},{17,16},{19,... | collective-permute-start | bytes 147464 | tf_op jit(solution)/shard_map/ppermute | solution.py:34
  31.4 7.1 %copy-start.6 = (f32[1,4,64,256]{3,2,1,0:T(8,128)}, f32[1,4,64,256]{3,2,1,0:T(8,128)S(1)}, u32[]{:S(2)}) copy-start(f32[1,4,64,256]{3,2,1,0:T(8,128)S(1)} %get-tuple-element.133) | copy-start | bytes 786436
  31.4 7.1 %copy-start.8 = (f32[1,4,64,256]{3,2,1,0:T(8,128)}, f32[1,4,64,256]{3,2,1,0:T(8,128)S(1)}, u32[]{:S(2)}) copy-start(f32[1,4,64,256]{3,2,1,0:T(8,128)S(1)} %get-tuple-element.134) | copy-start | bytes 786436
  31.4 7.1 %copy-start.10 = (f32[1,4,64,256]{3,2,1,0:T(8,128)}, f32[1,4,64,256]{3,2,1,0:T(8,128)S(1)}, u32[]{:S(2)}) copy-start(f32[1,4,64,256]{3,2,1,0:T(8,128)S(1)} %get-tuple-element.171) | copy-start | bytes 786436
  32.9 6.6 %copy-start.12 = (f32[1,4,64,256]{3,2,1,0:T(8,128)}, f32[1,4,64,256]{3,2,1,0:T(8,128)S(1)}, u32[]{:S(2)}) copy-start(f32[1,4,64,256]{3,2,1,0:T(8,128)S(1)} %get-tuple-element.141) | copy-start | bytes 786436
  32.9 6.6 %copy-start.14 = (f32[1,4,64,256]{3,2,1,0:T(8,128)}, f32[1,4,64,256]{3,2,1,0:T(8,128)S(1)}, u32[]{:S(2)}) copy-start(f32[1,4,64,256]{3,2,1,0:T(8,128)S(1)} %get-tuple-element.142) | copy-start | bytes 786436
  32.9 6.6 %copy-start.16 = (f32[1,4,64,256]{3,2,1,0:T(8,128)}, f32[1,4,64,256]{3,2,1,0:T(8,128)S(1)}, u32[]{:S(2)}) copy-start(f32[1,4,64,256]{3,2,1,0:T(8,128)S(1)} %get-tuple-element.175) | copy-start | bytes 786436
  33.0 6.6 %copy-start.18 = (f32[1,4,64,256]{3,2,1,0:T(8,128)}, f32[1,4,64,256]{3,2,1,0:T(8,128)S(1)}, u32[]{:S(2)}) copy-start(f32[1,4,64,256]{3,2,1,0:T(8,128)S(1)} %get-tuple-element.176) | copy-start | bytes 786436
  34.7 4.6 %copy-start.35 = (f32[1,4,64,256]{3,2,1,0:T(8,128)}, f32[1,4,64,256]{3,2,1,0:T(8,128)S(1)}, u32[]{:S(2)}) copy-start(f32[1,4,64,256]{3,2,1,0:T(8,128)S(1)} %get-tuple-element.149) | copy-start | bytes 786436
  34.7 4.6 %copy-start.36 = (f32[1,4,64,256]{3,2,1,0:T(8,128)}, f32[1,4,64,256]{3,2,1,0:T(8,128)S(1)}, u32[]{:S(2)}) copy-start(f32[1,4,64,256]{3,2,1,0:T(8,128)S(1)} %get-tuple-element.167) | copy-start | bytes 786436
  34.8 4.6 %copy-start.37 = (f32[1,4,64,256]{3,2,1,0:T(8,128)}, f32[1,4,64,256]{3,2,1,0:T(8,128)S(1)}, u32[]{:S(2)}) copy-start(f32[1,4,64,256]{3,2,1,0:T(8,128)S(1)} %get-tuple-element.168) | copy-start | bytes 786436
  35.4 3.6 %copy-start.38 = (f32[1,4,64,256]{3,2,1,0:T(8,128)}, f32[1,4,64,256]{3,2,1,0:T(8,128)S(1)}, u32[]{:S(2)}) copy-start(f32[1,4,64,256]{3,2,1,0:T(8,128)S(1)} %get-tuple-element.157) | copy-start | bytes 786436
  35.5 3.6 %copy-start.39 = (f32[1,4,64,256]{3,2,1,0:T(8,128)}, f32[1,4,64,256]{3,2,1,0:T(8,128)S(1)}, u32[]{:S(2)}) copy-start(f32[1,4,64,256]{3,2,1,0:T(8,128)S(1)} %get-tuple-element.169) | copy-start | bytes 786436
  36.1 2.5 %copy-start.20 = (f32[1,4,64,256]{3,2,1,0:T(8,128)}, f32[1,4,64,256]{3,2,1,0:T(8,128)S(1)}, u32[]{:S(2)}) copy-start(f32[1,4,64,256]{3,2,1,0:T(8,128)S(1)} %get-tuple-element.147) | copy-start | bytes 786436
  36.2 2.5 %copy-start.22 = (f32[1,4,64,256]{3,2,1,0:T(8,128)}, f32[1,4,64,256]{3,2,1,0:T(8,128)S(1)}, u32[]{:S(2)}) copy-start(f32[1,4,64,256]{3,2,1,0:T(8,128)S(1)} %get-tuple-element.148) | copy-start | bytes 786436
  36.2 2.5 %copy-start.24 = (f32[1,4,64,256]{3,2,1,0:T(8,128)}, f32[1,4,64,256]{3,2,1,0:T(8,128)S(1)}, u32[]{:S(2)}) copy-start(f32[1,4,64,256]{3,2,1,0:T(8,128)S(1)} %get-tuple-element.165) | copy-start | bytes 786436
  36.2 2.5 %copy-start.26 = (f32[1,4,64,256]{3,2,1,0:T(8,128)}, f32[1,4,64,256]{3,2,1,0:T(8,128)S(1)}, u32[]{:S(2)}) copy-start(f32[1,4,64,256]{3,2,1,0:T(8,128)S(1)} %get-tuple-element.166) | copy-start | bytes 786436
  45.2 5.1 %collective-permute-start.19 = (f32[3,6,2,256]{3,2,1,0:T(2,128)S(1)}, f32[3,6,2,256]{3,2,1,0:T(2,128)S(1)}, u32[]{:S(2)}, u32[]{:S(2)}) collective-permute-start(f32[3,6,2,256]{3,2,1,0:T(2,128)S(1)} %slice_select_fusion), channel_id=1, source_target_pairs={{0,1},{1,0},{2,3},{3,2},{4,5},{5,4},{6,7},{7,6},{8,9},{9,8},{10,11... | collective-permute-start | bytes 110600 | tf_op jit(solution)/shard_map/ppermute | solution.py:17
  50.1 2.4 %copy-start.5 = (f32[1,4,64,256]{3,2,1,0:T(8,128)S(1)}, f32[1,4,64,256]{3,2,1,0:T(8,128)}, u32[]{:S(2)}) copy-start(f32[1,4,64,256]{3,2,1,0:T(8,128)} %copy-done.4) | copy-start | bytes 786436
  50.1 2.4 %copy-start.7 = (f32[1,4,64,256]{3,2,1,0:T(8,128)S(1)}, f32[1,4,64,256]{3,2,1,0:T(8,128)}, u32[]{:S(2)}) copy-start(f32[1,4,64,256]{3,2,1,0:T(8,128)} %copy-done.6) | copy-start | bytes 786436
  50.5 18.0 %collective-permute-start.20 = (f32[3,2,64,256]{3,2,1,0:T(8,128)S(1)}, f32[3,2,64,256]{3,2,1,0:T(8,128)S(1)}, u32[]{:S(2)}, u32[]{:S(2)}) collective-permute-start(f32[3,2,64,256]{3,2,1,0:T(8,128)S(1)} %slice.812), channel_id=1, source_target_pairs={{0,2},{2,4},{4,6},{6,8},{8,10},{10,12},{12,14},{14,16},{16,18},{18... | collective-permute-start | bytes 1179656 | tf_op jit(solution)/shard_map/ppermute | solution.py:23
  56.2 12.4 %copy-start.44 = (f32[3,4,64,256]{3,2,1,0:T(8,128)S(1)}, f32[3,4,64,256]{3,2,1,0:T(8,128)}, u32[]{:S(2)}) copy-start(f32[3,4,64,256]{3,2,1,0:T(8,128)} %param.37) | copy-start | bytes 2359300
  69.0 16.6 %collective-permute-start.1 = (f32[6,64,256]{2,1,0:T(8,128)S(1)}, f32[6,64,256]{2,1,0:T(8,128)}, u32[]{:S(2)}, u32[]{:S(2)}) collective-permute-start(f32[6,64,256]{2,1,0:T(8,128)S(1)} %param.15), channel_id=1, source_target_pairs={{0,4},{4,0},{2,6},{6,2},{8,12},{12,8},{10,14},{14,10},{16,20},{20,... | collective-permute-start | bytes 1179656 | tf_op jit(solution)/shard_map/cond/branch_1_fun/ppermute | solution.py:17
  86.8 13.0 %collective-permute-start.4 = (f32[6,64,256]{2,1,0:T(8,128)S(1)}, f32[6,64,256]{2,1,0:T(8,128)}, u32[]{:S(2)}, u32[]{:S(2)}) collective-permute-start(f32[6,64,256]{2,1,0:T(8,128)S(1)} %param.18), channel_id=1, source_target_pairs={{0,2},{2,0},{4,6},{6,4},{8,10},{10,8},{12,14},{14,12},{16,18},{18,... | collective-permute-start | bytes 1179656 | tf_op jit(solution)/shard_map/cond/branch_0_fun/ppermute | solution.py:17
  100.9 46.1 %collective-permute-start.11 = (f32[6,64,256]{2,1,0:T(8,128)S(1)}, f32[6,64,256]{2,1,0:T(8,128)}, u32[]{:S(2)}, u32[]{:S(2)}) collective-permute-start(f32[6,64,256]{2,1,0:T(8,128)S(1)} %param.25), channel_id=1, source_target_pairs={{0,16},{16,0},{2,18},{18,2},{4,20},{20,4},{6,22},{22,6},{8,24},{24... | collective-permute-start | bytes 1179656 | tf_op jit(solution)/shard_map/cond/branch_3_fun/ppermute | solution.py:17
  148.2 30.5 %collective-permute-start.14 = (f32[6,64,256]{2,1,0:T(8,128)S(1)}, f32[6,64,256]{2,1,0:T(8,128)}, u32[]{:S(2)}, u32[]{:S(2)}) collective-permute-start(f32[6,64,256]{2,1,0:T(8,128)S(1)} %param.28), channel_id=1, source_target_pairs={{0,8},{8,0},{2,10},{10,2},{4,12},{12,4},{6,14},{14,6},{16,24},{24,... | collective-permute-start | bytes 1179656 | tf_op jit(solution)/shard_map/cond/branch_2_fun/ppermute | solution.py:17
  (24 other events, 43.5 us)
where the time goes:
time: 182 us; the launch traced here: 181 us
  waiting for transfers between devices  109 us (60%)
  starting transfers between devices  33.5 us (18%)
  other arithmetic  23 us (13%)
  between operations  10.7 us (6%)
  local copies, waits for them, and re-layouts  4.4 us (2%)
    ppermute x5, waiting for transfers between devices, from_partner(): return lax.ppermute(block, axis, route)  93.7 us
    ppermute x2, starting transfers between devices, shifted(): return lax.ppermute(block, axis, route)  15.8 us
    ppermute x5, starting transfers between devices, from_partner(): return lax.ppermute(block, axis, route)  15 us
    ppermute x2, waiting for transfers between devices, shifted(): return lax.ppermute(block, axis, route)  14.8 us
    add x1, other arithmetic, on_device(): reaction = reaction + placed  5.45 us
    mul x14, other arithmetic, bond_term(): return jnp.stack([factor * step_x, factor * step_y, factor * step_z])  4.31 us
  transfers between devices with their start and end apart: 9, of which 7 were waited for; matrix products, arithmetic and copies ran while one was open for 3% of the time, Pallas kernels for 0%

commit v1 on v0

v1 whole, which is shorter than its diff:
```python
import functools
import math

import jax
import jax.numpy as jnp
from jax import lax
from jax.experimental import pallas as pl
from jax.experimental.pallas import tpu as pltpu
from jax.sharding import PartitionSpec as P

GROUP = 16
LANES = 128
TOP = 8


def bond_table():
    table = []
    for step_x in range(-2, 3):
        for step_y in range(-2, 3):
            for step_z in range(-2, 3):
                square = step_x * step_x + step_y * step_y + step_z * step_z
                if 0 < square <= 4 and (step_x, step_y, step_z) > (0, 0, 0):
                    length = math.sqrt(square)
                    table.append((step_x, step_y, step_z, (1.0 - length / 2.5) / length**3))
    return table


BONDS = bond_table()


def to_groups(ref, component, rows, halves):
    group = rows // 4
    for half, value in enumerate(halves):
        low = component * 8 + half * 4
        ref[group, low : low + 4, :] = value[0:4]
        ref[group + 1, low : low + 4, :] = value[4:8]


def alive_of(flags, index):
    return (flags & (1 << (index % 8))) == 0


def pack_kernel(disp, damage, broken, up, down, edge, edge_up, edge_down, send):
    position = lax.axis_index("col")
    planes, rows = damage.shape[0], damage.shape[1]
    last = planes - 1
    for c in range(3):
        up[c] = disp[c, last]
        down[c] = disp[c, 0]
    up[3] = damage[last]
    up[4] = broken[0, last].astype(jnp.float32)
    up[5] = broken[1, last].astype(jnp.float32)
    up[6] = disp[0, last - 1]
    up[7] = jnp.where(alive_of(broken[1, last - 1], 15), damage[last - 1], 0.0)
    down[3] = damage[0]
    down[4] = disp[0, 1]
    down[5] = damage[1]
    edge_up[...] = jnp.zeros(edge_up.shape, jnp.float32)
    edge_down[...] = jnp.zeros(edge_down.shape, jnp.float32)

    def edges(first, inner):
        for plane in range(planes):
            at = slice(2 * plane, 2 * plane + 2)
            for c in range(3):
                edge[c, at] = disp[c, plane, first : first + 2]
            edge[3, at] = damage[plane, first : first + 2]
            for word in range(2):
                edge[4 + word, at] = broken[word, plane, first : first + 2].astype(jnp.float32)
        one = slice(inner, inner + 1)
        for c in range(3):
            edge_up[c : c + 1] = disp[c, last, one]
            edge_down[c : c + 1] = disp[c, 0, one]
        edge_up[3:4] = damage[last, one]
        edge_down[3:4] = damage[0, one]
        for word in range(2):
            edge_up[4 + word : 5 + word] = broken[word, last, one].astype(jnp.float32)

    @pl.when(position == 0)
    def _():
        edges(rows - 2, rows - 1)

    @pl.when(position == 1)
    def _():
        edges(0, 0)

    for c in range(3):
        for start in range(0, rows, 8):
            to_groups(
                send,
                c,
                start,
                [disp[c, 0, start : start + 8, h * LANES : (h + 1) * LANES] for h in range(2)],
            )


def fill(fields, flags, slot, values, words, rim, width, position, rows):
    lane = lax.broadcasted_iota(jnp.int32, (rows + 2 * TOP, LANES), 1)

    def base(ref, index, read, rim_read, dtype):
        ref[index, 2, slot, :, 0:TOP] = jnp.zeros((2, TOP, LANES), dtype)
        ref[index, 2, slot, :, TOP + rows :] = jnp.zeros((2, TOP, LANES), dtype)
        for half in range(2):
            cells = slice(half * LANES, (half + 1) * LANES)
            ref[index, 2, slot, half, TOP : TOP + rows] = read(cells)

        @pl.when(position == 0)
        def _():
            for half in range(2):
                cells = slice(half * LANES, (half + 1) * LANES)
                ref[index, 2, slot, half, TOP + rows : TOP + rows + width] = rim_read(cells)

        @pl.when(position == 1)
        def _():
            for half in range(2):
                cells = slice(half * LANES, (half + 1) * LANES)
                ref[index, 2, slot, half, TOP - width : TOP] = rim_read(cells)

    def shift(ref, index, amounts, zero):
        halves = [ref[index, 2, slot, half] for half in range(2)]
        for amount in amounts:
            rolled = [pltpu.roll(v, (-amount) % LANES, 1) for v in halves]
            crossed = lane >= LANES - amount if amount > 0 else lane < -amount
            edge = jnp.zeros_like(rolled[0]) if zero else rolled[0]
            if amount > 0:
                new = [jnp.where(crossed, rolled[1], rolled[0]), jnp.where(crossed, edge, rolled[1])]
            else:
                new = [jnp.where(crossed, edge, rolled[0]), jnp.where(crossed, rolled[0], rolled[1])]
            for half in range(2):
                ref[index, 2 + amount, slot, half] = new[half]

    for index, (read, rim_read) in enumerate(zip(values, rim[:4])):
        base(fields, index, read, rim_read, jnp.float32)
        shift(fields, index, (-2, -1, 1, 2) if index >= 2 else (-1, 1), index == 3)
    for index, (read, rim_read) in enumerate(zip(words, rim[4:])):
        base(flags, index, read, rim_read, jnp.int32)
        shift(flags, index, (-2, -1, 1) if index == 0 else (-1, 1), False)


def force_kernel(
    targets, disp, vel, damage, broken, up, down, edge, edge_up, edge_down, out, fields, flags
):
    position = lax.axis_index("col")
    planes, rows = damage.shape[0], damage.shape[1]
    needed = sorted({p + a for p in targets for a in (-1, 0, 1)})
    slots = {p: slot for slot, p in enumerate(needed)}

    for p in needed:
        if p < 0:
            values = [lambda cells, c=c: up[c, :, cells] for c in range(4)]
            words = [lambda cells, w=w: up[4 + w, :, cells].astype(jnp.int32) for w in range(2)]
            rim = [lambda cells, c=c: edge_up[c : c + 1, cells] for c in range(4)]
            rim += [
                lambda cells, w=w: edge_up[4 + w : 5 + w, cells].astype(jnp.int32) for w in range(2)
            ]
            width = 1
        elif p >= planes:
            values = [lambda cells, c=c: down[c, :, cells] for c in range(4)]
            words = []
            rim = [lambda cells, c=c: edge_down[c : c + 1, cells] for c in range(4)]
            width = 1
        else:
            at = slice(2 * p, 2 * p + 2)
            values = [lambda cells, c=c, p=p: disp[c, p, :, cells] for c in range(3)]
            values += [lambda cells, p=p: damage[p, :, cells]]
            words = [lambda cells, w=w, p=p: broken[w, p, :, cells] for w in range(2)]
            rim = [lambda cells, c=c, at=at: edge[c, at, cells] for c in range(4)]
            rim += [
                lambda cells, w=w, at=at: edge[4 + w, at, cells].astype(jnp.int32) for w in range(2)
            ]
            width = 2
        fill(fields, flags, slots[p], values, words, rim, width, position, rows)

    def block(step, carry):
        start = pl.multiple_of(step * 8, 8)
        own_rows = pl.ds(start, 8)
        for p in targets:
            updated = []
            for half in range(2):
                cells = slice(half * LANES, (half + 1) * LANES)
                own = [disp[c, p, own_rows, cells] for c in range(3)]
                own_damage = damage[p, own_rows, cells]
                own_words = [broken[w, p, own_rows, cells] for w in range(2)]
                force = [None, None, None]

                def add(axis, value):
                    force[axis] = value if force[axis] is None else force[axis] + value

                for index, (step_x, step_y, step_z, weight) in enumerate(BONDS):
                    for sign in (1, -1):
                        if step_x == 2:
                            q = p + 2 * sign
                            if q == -2:
                                other, scale = up[6, own_rows, cells], up[7, own_rows, cells]
                            elif q == -1:
                                other, scale = up[0, own_rows, cells], up[3, own_rows, cells]
                                bits = up[5, own_rows, cells].astype(jnp.int32)
                                scale = jnp.where(alive_of(bits, index), scale, 0.0)
                            elif q == planes + 1:
                                other, scale = down[4, own_rows, cells], down[5, own_rows, cells]
                            elif q == planes:
                                other, scale = down[0, own_rows, cells], down[3, own_rows, cells]
                            else:
                                other, scale = disp[0, q, own_rows, cells], damage[q, own_rows, cells]
                                if sign == -1:
                                    bits = broken[1, q, own_rows, cells]
                                    scale = jnp.where(alive_of(bits, index), scale, 0.0)
                            if sign == 1:
                                scale = jnp.where(alive_of(own_words[1], index), scale, 0.0)
                            factor = (4.0 * weight) * scale * (other - own[0])
                            add(0, factor)
                            continue
                        slot = slots[p + sign * step_x]
                        at = pl.ds(start + TOP + sign * step_y, 8)
                        place = 2 + sign * step_z
                        steps = (step_x, step_y, step_z)
                        along = None
                        for axis in range(3):
                            if steps[axis] == 0:
                                continue
                            part = fields[axis, place, slot, half, at] - own[axis]
                            if abs(steps[axis]) == 2:
                                along = part
                            elif along is None:
                                along = part if steps[axis] == 1 else -part
                            else:
                                along = along + part if steps[axis] == 1 else along - part
                        scale = fields[3, place, slot, half, at]
                        if sign == 1:
                            bits = own_words[index // 8]
                        else:
                            bits = flags[index // 8, place, slot, half, at]
                        scale = jnp.where(alive_of(bits, index), scale, 0.0)
                        if max(abs(s) for s in steps) == 2:
                            factor = (4.0 * weight) * scale * along
                        else:
                            factor = weight * scale * along
                        for axis in range(3):
                            if steps[axis] > 0:
                                add(axis, factor)
                            elif steps[axis] < 0:
                                add(axis, -factor)
                new_velocity = [
                    vel[c, p, own_rows, cells] + 0.1 * (own_damage * force[c]) for c in range(3)
                ]
                if targets == (0,):
                    updated.append(new_velocity)
                else:
                    for c in range(3):
                        out[3 + c, p, own_rows, cells] = new_velocity[c]
                        out[c, p, own_rows, cells] = own[c] + 0.1 * new_velocity[c]
            if targets == (0,):
                for c in range(3):
                    for half in range(2):
                        low = c * 8 + half * 4
                        out[2 * step, low : low + 4, :] = updated[half][c][0:4]
                        out[2 * step + 1, low : low + 4, :] = updated[half][c][4:8]
        return carry

    lax.fori_loop(0, rows // 8, block, 0)


def route_kernel(taken, bits, data, out, scratch):
    member = lax.rem(lax.axis_index("slab"), GROUP)
    column = 4 * member + lax.rem(lax.broadcasted_iota(jnp.int32, (24, LANES), 0), 4)
    for turn in range(4):
        source = data if turn == 0 else scratch.at[(turn - 1) % 2]
        target = out if turn == 3 else scratch.at[turn % 2]
        distance = jnp.left_shift(jnp.int32(1), bits[turn])
        for slab in range(GROUP):
            moved = column < taken[turn * GROUP + slab]
            target[slab] = jnp.where(moved, source[jnp.bitwise_xor(slab, distance)], source[slab])


def place_kernel(whole, first, second, out):
    del whole
    rows = out.shape[2]
    for start in range(0, rows, 8):
        group = start // 4
        at = slice(start, start + 8)
        for c in range(3):
            for half in range(2):
                cells = slice(half * LANES, (half + 1) * LANES)
                low = c * 8 + half * 4
                part = slice(low, low + 4)
                for g in range(2):
                    at = slice(start + 4 * g, start + 4 * g + 4)
                    velocity = second[group + g, part]
                    out[3 + c, 0, at, cells] = velocity
                    out[c, 0, at, cells] = first[group + g, part] + 0.1 * velocity


VMEM = pl.BlockSpec(memory_space=pltpu.VMEM)
SMEM = pl.BlockSpec(memory_space=pltpu.SMEM)
PARAMS = pltpu.CompilerParams(vmem_limit_bytes=40 * 1024 * 1024)


def exchange(block):
    count = lax.axis_size("slab")
    groups = [list(range(g, g + GROUP)) for g in range(0, count, GROUP)]
    return lax.all_to_all(block, "slab", 0, 0, axis_index_groups=groups)


def on_device(displacement, velocity, damage, broken, counts, bits):
    planes, rows, cells = damage.shape
    f32 = jnp.float32
    shape = jax.ShapeDtypeStruct
    group_shape = (GROUP, 24, LANES)
    up, down, edge, edge_up, edge_down, first = pl.pallas_call(
        pack_kernel,
        out_shape=[
            shape((8, rows, cells), f32),
            shape((6, rows, cells), f32),
            shape((6, 2 * planes, cells), f32),
            shape((8, cells), f32),
            shape((8, cells), f32),
            shape(group_shape, f32),
        ],
        in_specs=[VMEM] * 3,
        out_specs=[VMEM] * 6,
        compiler_params=PARAMS,
        name="pack",
    )(displacement, damage, broken)

    slabs = lax.axis_size("slab")
    upward = [(i, i + 1) for i in range(slabs - 1)]
    downward = [(i + 1, i) for i in range(slabs - 1)]
    across_up = [(2 * s + c, 2 * t + 1 - c) for s, t in upward for c in range(2)]
    across_down = [(2 * s + c, 2 * t + 1 - c) for s, t in downward for c in range(2)]
    both = ("slab", "col")
    up = lax.ppermute(up, "slab", upward)
    edge_up = lax.ppermute(edge_up, both, across_up)
    edge = lax.ppermute(edge, "col", [(0, 1), (1, 0)])
    down = lax.ppermute(down, "slab", downward)
    edge_down = lax.ppermute(edge_down, both, across_down)

    member = jnp.arange(GROUP, dtype=jnp.int32)
    base = lax.axis_index("slab") // GROUP * GROUP
    mine = lax.dynamic_slice_in_dim(counts, base, GROUP, 0).T
    partner = jnp.bitwise_xor(member[None, :], jnp.left_shift(jnp.int32(1), bits)[:, None])
    taken = jnp.minimum(mine, jnp.take_along_axis(mine, partner, axis=1)).reshape(-1)

    def forces(targets, out):
        kept = len(targets) + 2
        return pl.pallas_call(
            functools.partial(force_kernel, targets),
            out_shape=out,
            in_specs=[VMEM] * 9,
            out_specs=VMEM,
            scratch_shapes=[
                pltpu.VMEM((4, 5, kept, 2, rows + 2 * TOP, LANES), f32),
                pltpu.VMEM((2, 5, kept, 2, rows + 2 * TOP, LANES), jnp.int32),
            ],
            compiler_params=PARAMS,
            name="force_first" if targets == (0,) else "force_rest",
        )(displacement, velocity, damage, broken, up, down, edge, edge_up, edge_down)

    def route(data):
        return pl.pallas_call(
            route_kernel,
            out_shape=shape(group_shape, f32),
            in_specs=[SMEM, SMEM, VMEM],
            out_specs=VMEM,
            scratch_shapes=[pltpu.VMEM((2,) + group_shape, f32)],
            compiler_params=PARAMS,
            name="route",
        )(taken, bits, data)

    second = forces((0,), shape(group_shape, f32))
    whole = forces(tuple(range(1, planes)), shape((6, planes, rows, cells), f32))
    first = exchange(route(exchange(first)))
    second = exchange(route(exchange(second)))
    return pl.pallas_call(
        place_kernel,
        out_shape=shape((6, planes, rows, cells), f32),
        in_specs=[pl.BlockSpec(memory_space=pl.ANY)] + [pl.BlockSpec(group_shape, lambda i: (0, 0, 0))] * 2,
        out_specs=pl.BlockSpec((6, 1, rows, cells), lambda i: (0, 0, 0, 0)),
        grid=(1,),
        input_output_aliases={0: 0},
        compiler_params=PARAMS,
        name="place",
    )(whole, first, second)


def solution(mesh):
    return jax.shard_map(
        on_device,
        mesh=mesh,
        in_specs=(
            P(None, "slab", "col", None),
            P(None, "slab", "col", None),
            P("slab", "col", None),
            P(None, "slab", "col", None),
            P(),
            P(),
        ),
        out_specs=P(None, "slab", "col", None),
        check_vma=False,
    )
```

time: 182 us -> 120 us (0.66)
  waiting for transfers between devices: 109 us -> 39.4 us
  other arithmetic: 23 us -> 0.86 us
  starting transfers between devices: 33.5 us -> 55 us
  Pallas kernels: 0 us -> 15.9 us
  between operations: 10.7 us -> 0.2 us
  local copies, waits for them, and re-layouts: 4.4 us -> 7.91 us
    ppermute x9 -> x5, waiting for transfers between devices: 109 us -> 3.84 us  [the longest x1 3.08 us: on_device(): edge_up = lax.ppermute(edge_up, both, across_up)]
    all_to_all x0 -> x4, waiting for transfers between devices: none -> 35.6 us  [exchange(): return lax.all_to_all(block, 'slab', 0, 0, axis_index_groups=groups)]
    all_to_all x0 -> x4, starting transfers between devices: none -> 33.2 us  [exchange(): return lax.all_to_all(block, 'slab', 0, 0, axis_index_groups=groups)]
    pallas_call x0 -> x6, Pallas kernels: none -> 15.9 us  [the longest x2 11.7 us: forces(): pl.pallas_call(functools.partial(force_kernel, targets), out_shape=out, i...]
    ppermute x9 -> x5, starting transfers between devices: 33.5 us -> 21.8 us  [the longest x1 7.86 us: on_device(): edge_down = lax.ppermute(edge_down, both, across_down)]
    add x3 -> x0, other arithmetic: 9.17 us -> none  [the longest x1 5.45 us: on_device(): reaction = reaction + placed]
    unnamed x94 -> x28, local copies, waits for them, and re-layouts: 1.85 us -> 6.7 us
    mul x14 -> x0, other arithmetic: 4.31 us -> none  [bond_term(): return jnp.stack([factor * step_x, factor * step_y, factor * step_z])]
  transfers between devices with their start and end apart: 9 -> 9, of which waited for: 7 -> 5; matrix products, arithmetic and copies ran while one was open for 3% -> 2% of each run, Pallas kernels for 0% -> 11%
where the time goes in v1:
time: 120 us; the launch traced here: 119 us
  starting transfers between devices  55 us (46%)
  waiting for transfers between devices  39.4 us (33%)
  Pallas kernels  15.9 us (13%)
  local copies, waits for them, and re-layouts  7.91 us (7%)
    all_to_all x4, waiting for transfers between devices, exchange(): return lax.all_to_all(block, 'slab', 0, 0, axis_index_groups=groups)  35.6 us
    all_to_all x4, starting transfers between devices, exchange(): return lax.all_to_all(block, 'slab', 0, 0, axis_index_groups=groups)  33.2 us
    pallas_call x2, Pallas kernels, forces(): pl.pallas_call(functools.partial(force_kernel, targets), out_shape=out, i...  11.7 us
    ppermute x1, starting transfers between devices, on_device(): edge_down = lax.ppermute(edge_down, both, across_down)  7.86 us
    unnamed x28, local copies, waits for them, and re-layouts  6.7 us
    ppermute x1, starting transfers between devices, on_device(): down = lax.ppermute(down, 'slab', downward)  6.24 us
    ppermute x1, starting transfers between devices, on_device(): up = lax.ppermute(up, 'slab', upward)  3.82 us
    ppermute x1, waiting for transfers between devices, on_device(): edge_up = lax.ppermute(edge_up, both, across_up)  3.08 us
  transfers between devices with their start and end apart: 9, of which 5 were waited for; matrix products, arithmetic and copies ran while one was open for 2% of the time, Pallas kernels for 11%

profile of v1, /device:TPU:24, one launch (start us, length us, event | category | flops | bytes accessed | tf_op | source)
XLA Modules:
  0.0 119.3 jit_solution(4328259904067876833)
XLA Ops:
  0.0 1.1 copy-done
  1.1 1.0 copy-done.2
  2.2 0.9 copy-done.6
  3.1 0.8 pack.1
  3.9 0.7 copy-done.11
  4.7 15.2 %all-to-all-start = ((f32[16,24,128]{2,1,0:T(8,128)}), f32[16,24,128]{2,1,0:T(8,128)S(1)}, u32[]{:S(2)}, u32[]{:S(2)}) async-start(f32[16,24,128]{2,1,0:T(8,128)} %get-tuple-element.16), calls=%async_computation | async-start | bytes 393216 | tf_op jit(solution)/shard_map/all_to_all | solution.py:300
  19.9 3.8 %collective-permute-start = (f32[8,64,256]{2,1,0:T(8,128)S(1)}, f32[8,64,256]{2,1,0:T(8,128)S(1)}, u32[]{:S(2)}, u32[]{:S(2)}) collective-permute-start(f32[8,64,256]{2,1,0:T(8,128)S(1)} %get-tuple-element.11), channel_id=1, source_target_pairs={{0,2},{2,4},{4,6},{6,8},{8,10},{10,12},{12,14},{14,16},{16,18},{18... | collective-permute-start | bytes 1572872 | tf_op jit(solution)/shard_map/ppermute | solution.py:330
  23.7 6.2 %collective-permute-start.1 = (f32[6,64,256]{2,1,0:T(8,128)}, f32[6,64,256]{2,1,0:T(8,128)S(1)}, u32[]{:S(2)}, u32[]{:S(2)}) collective-permute-start(f32[6,64,256]{2,1,0:T(8,128)} %copy-done.11), channel_id=1, source_target_pairs={{2,0},{4,2},{6,4},{8,6},{10,8},{12,10},{14,12},{16,14},{18,16},{20... | collective-permute-start | bytes 1179656 | tf_op jit(solution)/shard_map/ppermute | solution.py:333
  29.9 1.9 %collective-permute-start.2 = (f32[6,8,256]{2,1,0:T(8,128)S(1)}, f32[6,8,256]{2,1,0:T(8,128)S(1)}, u32[]{:S(2)}, u32[]{:S(2)}) collective-permute-start(f32[6,8,256]{2,1,0:T(8,128)S(1)} %get-tuple-element.13), channel_id=1, source_target_pairs={{0,1},{1,0},{2,3},{3,2},{4,5},{5,4},{6,7},{7,6},{8,9},{9,8},{10,11... | collective-permute-start | bytes 147464 | tf_op jit(solution)/shard_map/ppermute | solution.py:332
  31.9 1.9 %collective-permute-start.3 = (f32[8,256]{1,0:T(8,128)S(1)}, f32[8,256]{1,0:T(8,128)S(1)}, u32[]{:S(2)}, u32[]{:S(2)}) collective-permute-start(f32[8,256]{1,0:T(8,128)S(1)} %get-tuple-element.14), channel_id=1, source_target_pairs={{0,3},{1,2},{2,5},{3,4},{4,7},{5,6},{6,9},{7,8},{8,11},{9,10},{10,... | collective-permute-start | bytes 24584 | tf_op jit(solution)/shard_map/ppermute | solution.py:331
  33.8 7.9 %collective-permute-start.4 = (f32[8,256]{1,0:T(8,128)S(1)}, f32[8,256]{1,0:T(8,128)S(1)}, u32[]{:S(2)}, u32[]{:S(2)}) collective-permute-start(f32[8,256]{1,0:T(8,128)S(1)} %get-tuple-element.15), channel_id=1, source_target_pairs={{2,1},{3,0},{4,3},{5,2},{6,5},{7,4},{8,7},{9,6},{10,9},{11,8},{12,... | collective-permute-start | bytes 24584 | tf_op jit(solution)/shard_map/ppermute | solution.py:334
  41.7 3.1 %collective-permute-done.3.edge_up = f32[8,256]{1,0:T(8,128)S(1)} collective-permute-done((f32[8,256]{1,0:T(8,128)S(1)}, f32[8,256]{1,0:T(8,128)S(1)}, u32[]{:S(2)}, u32[]{:S(2)}) %collective-permute-start.3) | collective-permute-done | bytes 8224 | tf_op jit(solution)/shard_map/ppermute | solution.py:331
  44.8 0.7 collective-permute-done.up
  45.6 1.1 copy-done.4
  46.7 4.0 %force_first.1 = f32[16,24,128]{2,1,0:T(8,128)} custom-call(f32[3,4,64,256]{3,2,1,0:T(8,128)S(1)} %copy-done.1, f32[3,4,64,256]{3,2,1,0:T(8,128)S(1)} %copy-done.4, f32[4,64,256]{2,1,0:T(8,128)S(1)} %copy-done.7, s32[2,4,64,256]{3,2,1,0:T(8,128)S(1)} %copy-done.3, f32[8,64,256]{2,1,0:T(8,128)S(1)} %collective-permute-done.up, ...), custom_call_target="tpu_custom_call" | custom-call | tf_op jit(solution)/shard_map/force_first/pallas_call | solution.py:344
  50.7 7.0 %all-to-all-start.2 = ((f32[16,24,128]{2,1,0:T(8,128)}), f32[16,24,128]{2,1,0:T(8,128)}, u32[]{:S(2)}, u32[]{:S(2)}) async-start(f32[16,24,128]{2,1,0:T(8,128)} %force_first.1), calls=%async_computation.2 | async-start | bytes 393216 | tf_op jit(solution)/shard_map/all_to_all | solution.py:300
  57.9 0.1 reshape.62
  57.9 0.3 copy-done.13
  58.4 0.9 gather_fusion
  59.2 0.1 reshape.65
  59.3 0.8 select_minimum_fusion
  60.2 0.7 route.2
  60.9 0.7 copy-done.9
  61.5 12.0 %all-to-all-done.2.data = f32[16,24,128]{2,1,0:T(8,128)} async-done(((f32[16,24,128]{2,1,0:T(8,128)}), f32[16,24,128]{2,1,0:T(8,128)}, u32[]{:S(2)}, u32[]{:S(2)}) %all-to-all-start.2) | async-done | bytes 196640 | tf_op jit(solution)/shard_map/all_to_all | solution.py:300
  73.5 6.0 %all-to-all-start.1 = ((f32[16,24,128]{2,1,0:T(8,128)}), f32[16,24,128]{2,1,0:T(8,128)S(1)}, u32[]{:S(2)}, u32[]{:S(2)}) async-start(f32[16,24,128]{2,1,0:T(8,128)} %copy-done.9), calls=%async_computation.1 | async-start | bytes 393216 | tf_op jit(solution)/shard_map/all_to_all | solution.py:300
  79.6 1.1 route.3
  80.7 0.7 copy-done.8
  81.3 14.7 %all-to-all-done.1.first = f32[16,24,128]{2,1,0:T(8,128)S(1)} async-done(((f32[16,24,128]{2,1,0:T(8,128)}), f32[16,24,128]{2,1,0:T(8,128)S(1)}, u32[]{:S(2)}, u32[]{:S(2)}) %all-to-all-start.1) | async-done | bytes 196640 | tf_op jit(solution)/shard_map/all_to_all | solution.py:300
  96.1 4.9 %all-to-all-start.3 = ((f32[16,24,128]{2,1,0:T(8,128)}), f32[16,24,128]{2,1,0:T(8,128)}, u32[]{:S(2)}, u32[]{:S(2)}) async-start(f32[16,24,128]{2,1,0:T(8,128)} %copy-done.8), calls=%async_computation.3 | async-start | bytes 393216 | tf_op jit(solution)/shard_map/all_to_all | solution.py:300
  101.0 7.6 %force_rest.1.whole = f32[6,4,64,256]{3,2,1,0:T(8,128)} custom-call(f32[3,4,64,256]{3,2,1,0:T(8,128)S(1)} %copy-done.1, f32[3,4,64,256]{3,2,1,0:T(8,128)S(1)} %copy-done.5, f32[4,64,256]{2,1,0:T(8,128)S(1)} %copy-done.7, s32[2,4,64,256]{3,2,1,0:T(8,128)S(1)} %copy-done.3, f32[8,64,256]{2,1,0:T(8,128)S(1)} %collective-permute-done.up, ...), custom_call_target="tpu_custom_call" | custom-call | tf_op jit(solution)/shard_map/force_rest/pallas_call | solution.py:344
  108.7 8.9 %all-to-all-done.3.second = f32[16,24,128]{2,1,0:T(8,128)} async-done(((f32[16,24,128]{2,1,0:T(8,128)}), f32[16,24,128]{2,1,0:T(8,128)}, u32[]{:S(2)}, u32[]{:S(2)}) %all-to-all-start.3) | async-done | bytes 196640 | tf_op jit(solution)/shard_map/all_to_all | solution.py:300
  117.5 1.8 %place.1 = f32[6,4,64,256]{3,2,1,0:T(8,128)} custom-call(f32[6,4,64,256]{3,2,1,0:T(8,128)} %force_rest.1.whole, f32[16,24,128]{2,1,0:T(8,128)S(1)} %all-to-all-done.1.first, f32[16,24,128]{2,1,0:T(8,128)} %all-to-all-done.3.second), custom_call_target="tpu_custom_call", output_to_operand_aliasing={{}: (0, {})} | custom-call | tf_op jit(solution)/shard_map/place/pallas_call | solution.py:372
  (28 shorter events, 0.3 us)
Async XLA Ops:
  0.0 1.1 copy-start
  1.1 1.0 copy-start.2
  2.2 0.9 copy-start.6
  3.1 42.4 %copy-start.1 = (f32[3,4,64,256]{3,2,1,0:T(8,128)S(1)}, f32[3,4,64,256]{3,2,1,0:T(8,128)}, u32[]{:S(2)}) copy-start(f32[3,4,64,256]{3,2,1,0:T(8,128)} %disp.5) | copy-start | bytes 2359300
  3.1 42.4 %copy-start.3 = (s32[2,4,64,256]{3,2,1,0:T(8,128)S(1)}, s32[2,4,64,256]{3,2,1,0:T(8,128)}, u32[]{:S(2)}) copy-start(s32[2,4,64,256]{3,2,1,0:T(8,128)} %broken.5) | copy-start | bytes 1572868
  3.1 42.4 %copy-start.7 = (f32[4,64,256]{2,1,0:T(8,128)S(1)}, f32[4,64,256]{2,1,0:T(8,128)}, u32[]{:S(2)}) copy-start(f32[4,64,256]{2,1,0:T(8,128)} %damage.5) | copy-start | bytes 786436
  3.9 0.7 copy-start.11
  4.7 46.1 %all-to-all-start = ((f32[16,24,128]{2,1,0:T(8,128)}), f32[16,24,128]{2,1,0:T(8,128)S(1)}, u32[]{:S(2)}, u32[]{:S(2)}) async-start(f32[16,24,128]{2,1,0:T(8,128)} %get-tuple-element.16), calls=%async_computation | async-start | bytes 393216 | tf_op jit(solution)/shard_map/all_to_all | solution.py:300
  19.9 25.7 %collective-permute-start = (f32[8,64,256]{2,1,0:T(8,128)S(1)}, f32[8,64,256]{2,1,0:T(8,128)S(1)}, u32[]{:S(2)}, u32[]{:S(2)}) collective-permute-start(f32[8,64,256]{2,1,0:T(8,128)S(1)} %get-tuple-element.11), channel_id=1, source_target_pairs={{0,2},{2,4},{4,6},{6,8},{8,10},{10,12},{12,14},{14,16},{16,18},{18... | collective-permute-start | bytes 1572872 | tf_op jit(solution)/shard_map/ppermute | solution.py:330
  23.7 21.1 %collective-permute-start.1 = (f32[6,64,256]{2,1,0:T(8,128)}, f32[6,64,256]{2,1,0:T(8,128)S(1)}, u32[]{:S(2)}, u32[]{:S(2)}) collective-permute-start(f32[6,64,256]{2,1,0:T(8,128)} %copy-done.11), channel_id=1, source_target_pairs={{2,0},{4,2},{6,4},{8,6},{10,8},{12,10},{14,12},{16,14},{18,16},{20... | collective-permute-start | bytes 1179656 | tf_op jit(solution)/shard_map/ppermute | solution.py:333
  29.9 14.9 %collective-permute-start.2 = (f32[6,8,256]{2,1,0:T(8,128)S(1)}, f32[6,8,256]{2,1,0:T(8,128)S(1)}, u32[]{:S(2)}, u32[]{:S(2)}) collective-permute-start(f32[6,8,256]{2,1,0:T(8,128)S(1)} %get-tuple-element.13), channel_id=1, source_target_pairs={{0,1},{1,0},{2,3},{3,2},{4,5},{5,4},{6,7},{7,6},{8,9},{9,8},{10,11... | collective-permute-start | bytes 147464 | tf_op jit(solution)/shard_map/ppermute | solution.py:332
  31.9 12.9 %collective-permute-start.3 = (f32[8,256]{1,0:T(8,128)S(1)}, f32[8,256]{1,0:T(8,128)S(1)}, u32[]{:S(2)}, u32[]{:S(2)}) collective-permute-start(f32[8,256]{1,0:T(8,128)S(1)} %get-tuple-element.14), channel_id=1, source_target_pairs={{0,3},{1,2},{2,5},{3,4},{4,7},{5,6},{6,9},{7,8},{8,11},{9,10},{10,... | collective-permute-start | bytes 24584 | tf_op jit(solution)/shard_map/ppermute | solution.py:331
  33.8 11.0 %collective-permute-start.4 = (f32[8,256]{1,0:T(8,128)S(1)}, f32[8,256]{1,0:T(8,128)S(1)}, u32[]{:S(2)}, u32[]{:S(2)}) collective-permute-start(f32[8,256]{1,0:T(8,128)S(1)} %get-tuple-element.15), channel_id=1, source_target_pairs={{2,1},{3,0},{4,3},{5,2},{6,5},{7,4},{8,7},{9,6},{10,9},{11,8},{12,... | collective-permute-start | bytes 24584 | tf_op jit(solution)/shard_map/ppermute | solution.py:334
  41.7 16.6 %copy-start.12 = (s32[256,4]{0,1:T(4,128)S(1)}, s32[256,4]{0,1:T(4,128)}, u32[]{:S(2)}) copy-start(s32[256,4]{0,1:T(4,128)} %param.10) | copy-start | bytes 12292
  41.7 16.1 %copy-start.10 = (s32[4]{0:T(128)S(1)}, s32[4]{0:T(128)}, u32[]{:S(2)}) copy-start(s32[4]{0:T(128)} %bits.3) | copy-start | bytes 52
  45.6 1.1 copy-start.4
  50.7 22.8 %all-to-all-start.2 = ((f32[16,24,128]{2,1,0:T(8,128)}), f32[16,24,128]{2,1,0:T(8,128)}, u32[]{:S(2)}, u32[]{:S(2)}) async-start(f32[16,24,128]{2,1,0:T(8,128)} %force_first.1), calls=%async_computation.2 | async-start | bytes 393216 | tf_op jit(solution)/shard_map/all_to_all | solution.py:300
  57.8 0.5 copy-start.13
  58.4 42.7 %copy-start.5 = (f32[3,4,64,256]{3,2,1,0:T(8,128)S(1)}, f32[3,4,64,256]{3,2,1,0:T(8,128)}, u32[]{:S(2)}) copy-start(f32[3,4,64,256]{3,2,1,0:T(8,128)} %vel.3) | copy-start | bytes 2359300
  60.9 0.7 copy-start.9
  73.5 22.5 %all-to-all-start.1 = ((f32[16,24,128]{2,1,0:T(8,128)}), f32[16,24,128]{2,1,0:T(8,128)S(1)}, u32[]{:S(2)}, u32[]{:S(2)}) async-start(f32[16,24,128]{2,1,0:T(8,128)} %copy-done.9), calls=%async_computation.1 | async-start | bytes 393216 | tf_op jit(solution)/shard_map/all_to_all | solution.py:300
  80.6 0.7 copy-start.8
  96.1 21.5 %all-to-all-start.3 = ((f32[16,24,128]{2,1,0:T(8,128)}), f32[16,24,128]{2,1,0:T(8,128)}, u32[]{:S(2)}, u32[]{:S(2)}) async-start(f32[16,24,128]{2,1,0:T(8,128)} %copy-done.8), calls=%async_computation.3 | async-start | bytes 393216 | tf_op jit(solution)/shard_map/all_to_all | solution.py:300

commit v2 on v1

--- a/solution.py
+++ b/solution.py
@@ -28,69 +28,88 @@
 BONDS = bond_table()
 
 
-def to_groups(ref, component, rows, halves):
-    group = rows // 4
-    for half, value in enumerate(halves):
-        low = component * 8 + half * 4
-        ref[group, low : low + 4, :] = value[0:4]
-        ref[group + 1, low : low + 4, :] = value[4:8]
+def to_groups(ref, step, first, half, values):
+    for c, value in enumerate(values):
+        low = (first + c) * 8 + half * 4
+        ref[2 * step, low : low + 4, :] = value[0:4]
+        ref[2 * step + 1, low : low + 4, :] = value[4:8]
 
 
 def alive_of(flags, index):
     return (flags & (1 << (index % 8))) == 0
 
 
-def pack_kernel(disp, damage, broken, up, down, edge, edge_up, edge_down, send):
+def pack_up_kernel(disp, damage, broken, up, words, scale, sems):
+    last = damage.shape[0] - 1
+    moves = [(disp.at[c, last], up.at[c]) for c in range(3)]
+    moves += [(damage.at[last], up.at[3]), (disp.at[0, last - 1], up.at[6])]
+    moves += [(broken.at[w, last], words.at[w]) for w in range(2)]
+    moves += [(broken.at[1, last - 1], words.at[2]), (damage.at[last - 1], scale)]
+    copies = [
+        pltpu.make_async_copy(source, target, sems.at[i])
+        for i, (source, target) in enumerate(moves)
+    ]
+    for copy in copies:
+        copy.start()
+    for copy in copies:
+        copy.wait()
+    up[4] = words[0].astype(jnp.float32)
+    up[5] = words[1].astype(jnp.float32)
+    up[7] = jnp.where(alive_of(words[2], 15), scale[...], 0.0)
+
+
+def pack_rest_kernel(
+    disp, damage, broken, order, down, edge, edge_up, edge_down, disp_rim, damage_rim, words, sems
+):
+    del order
     position = lax.axis_index("col")
     planes, rows = damage.shape[0], damage.shape[1]
     last = planes - 1
-    for c in range(3):
-        up[c] = disp[c, last]
-        down[c] = disp[c, 0]
-    up[3] = damage[last]
-    up[4] = broken[0, last].astype(jnp.float32)
-    up[5] = broken[1, last].astype(jnp.float32)
-    up[6] = disp[0, last - 1]
-    up[7] = jnp.where(alive_of(broken[1, last - 1], 15), damage[last - 1], 0.0)
-    down[3] = damage[0]
-    down[4] = disp[0, 1]
-    down[5] = damage[1]
+    rim = pl.ds(pl.multiple_of((1 - position) * (rows - 8), 8), 8)
+    moves = [
+        (disp.at[:, :, rim], disp_rim),
+        (damage.at[:, rim], damage_rim),
+        (broken.at[:, :, rim], words),
+        (disp.at[0, 1], down.at[4]),
+        (damage.at[0], down.at[3]),
+        (damage.at[1], down.at[5]),
+    ]
+    moves += [(disp.at[c, 0], down.at[c]) for c in range(3)]
+    copies = [
+        pltpu.make_async_copy(source, target, sems.at[i])
+        for i, (source, target) in enumerate(moves)
+    ]
+    for copy in copies:
+        copy.start()
     edge_up[...] = jnp.zeros(edge_up.shape, jnp.float32)
     edge_down[...] = jnp.zeros(edge_down.shape, jnp.float32)
+    for copy in copies:
+        copy.wait()
 
     def edges(first, inner):
         for plane in range(planes):
             at = slice(2 * plane, 2 * plane + 2)
             for c in range(3):
-                edge[c, at] = disp[c, plane, first : first + 2]
-            edge[3, at] = damage[plane, first : first + 2]
+                edge[c, at] = disp_rim[c, plane, first : first + 2]
+            edge[3, at] = damage_rim[plane, first : first + 2]
             for word in range(2):
-                edge[4 + word, at] = broken[word, plane, first : first + 2].astype(jnp.float32)
+                edge[4 + word, at] = words[word, plane, first : first + 2].astype(jnp.float32)
         one = slice(inner, inner + 1)
         for c in range(3):
-            edge_up[c : c + 1] = disp[c, last, one]
-            edge_down[c : c + 1] = disp[c, 0, one]
-        edge_up[3:4] = damage[last, one]
-        edge_down[3:4] = damage[0, one]
+            edge_up[c : c + 1] = disp_rim[c, last, one]
+            edge_down[c : c + 1] = disp_rim[c, 0, one]
+        edge_up[3:4] = damage_rim[last, one]
+        edge_down[3:4] = damage_rim[0, one]
         for word in range(2):
-            edge_up[4 + word : 5 + word] = broken[word, last, one].astype(jnp.float32)
+            edge_up[4 + word : 5 + word] = words[word, last, one].astype(jnp.float32)
 
     @pl.when(position == 0)
     def _():
-        edges(rows - 2, rows - 1)
+        edges(6, 7)
 
     @pl.when(position == 1)
     def _():
         edges(0, 0)
-
-    for c in range(3):
-        for start in range(0, rows, 8):
-            to_groups(
-                send,
-                c,
-                start,
-                [disp[c, 0, start : start + 8, h * LANES : (h + 1) * LANES] for h in range(2)],
-            )
 
 
 def fill(fields, flags, slot, values, words, rim, width, position, rows):
@@ -136,12 +155,16 @@
         shift(flags, index, (-2, -1, 1) if index == 0 else (-1, 1), False)
 
 
-def force_kernel(
-    targets, disp, vel, damage, broken, up, down, edge, edge_up, edge_down, out, fields, flags
-):
+def force_kernel(targets, low, high, names, *refs):
+    ref_of = dict(zip(names, refs))
+    out, fields, flags = refs[len(names) :]
+    disp, vel, damage = ref_of["disp"], ref_of["vel"], ref_of["damage"]
+    broken, up, down = ref_of.get("broken"), ref_of.get("up"), ref_of.get("down")
+    edge, edge_up, edge_down = ref_of.get("edge"), ref_of.get("edge_up"), ref_of.get("edge_down")
     position = lax.axis_index("col")
-    planes, rows = damage.shape[0], damage.shape[1]
-    needed = sorted({p + a for p in targets for a in (-1, 0, 1)})
+    planes, rows = ref_of["damage"].shape[0], damage.shape[1]
+    closing = high == 0
+    needed = sorted({p + a for p in targets for a in (-1, 0, 1) if low <= p + a < high})
     slots = {p: slot for slot, p in enumerate(needed)}
 
     for p in needed:
@@ -174,12 +197,11 @@
         start = pl.multiple_of(step * 8, 8)
         own_rows = pl.ds(start, 8)
         for p in targets:
-            updated = []
             for half in range(2):
                 cells = slice(half * LANES, (half + 1) * LANES)
                 own = [disp[c, p, own_rows, cells] for c in range(3)]
                 own_damage = damage[p, own_rows, cells]
-                own_words = [broken[w, p, own_rows, cells] for w in range(2)]
+                own_words = [broken[w, p, own_rows, cells] for w in range(2)] if not closing else []
                 force = [None, None, None]
 
                 def add(axis, value):
@@ -187,6 +209,8 @@
 
                 for index, (step_x, step_y, step_z, weight) in enumerate(BONDS):
                     for sign in (1, -1):
+                        if not low <= p + sign * step_x < high:
+                            continue
                         if step_x == 2:
                             q = p + 2 * sign
                             if q == -2:
@@ -242,18 +266,16 @@
                 new_velocity = [
                     vel[c, p, own_rows, cells] + 0.1 * (own_damage * force[c]) for c in range(3)
                 ]
-                if targets == (0,):
-                    updated.append(new_velocity)
+                if closing:
+                    to_groups(out, step, 0, half, new_velocity)
+                    to_groups(out, step, 3, half, own)
+                elif targets == (0,):
+                    for c in range(3):
+                        out[c, 0, own_rows, cells] = new_velocity[c]
                 else:
                     for c in range(3):
                         out[3 + c, p, own_rows, cells] = new_velocity[c]
                         out[c, p, own_rows, cells] = own[c] + 0.1 * new_velocity[c]
-            if targets == (0,):
-                for c in range(3):
-                    for half in range(2):
-                        low = c * 8 + half * 4
-                        out[2 * step, low : low + 4, :] = updated[half][c][0:4]
-                        out[2 * step + 1, low : low + 4, :] = updated[half][c][4:8]
         return carry
 
     lax.fori_loop(0, rows // 8, block, 0)
@@ -261,7 +283,7 @@
 
 def route_kernel(taken, bits, data, out, scratch):
     member = lax.rem(lax.axis_index("slab"), GROUP)
-    column = 4 * member + lax.rem(lax.broadcasted_iota(jnp.int32, (24, LANES), 0), 4)
+    column = 4 * member + lax.rem(lax.broadcasted_iota(jnp.int32, (48, LANES), 0), 4)
     for turn in range(4):
         source = data if turn == 0 else scratch.at[(turn - 1) % 2]
         target = out if turn == 3 else scratch.at[turn % 2]
@@ -271,7 +293,7 @@
             target[slab] = jnp.where(moved, source[jnp.bitwise_xor(slab, distance)], source[slab])
 
 
-def place_kernel(whole, first, second, out):
+def place_kernel(whole, columns, out):
     del whole
     rows = out.shape[2]
     for start in range(0, rows, 8):
@@ -284,13 +306,14 @@
                 part = slice(low, low + 4)
                 for g in range(2):
                     at = slice(start + 4 * g, start + 4 * g + 4)
-                    velocity = second[group + g, part]
+                    velocity = columns[group + g, part]
                     out[3 + c, 0, at, cells] = velocity
-                    out[c, 0, at, cells] = first[group + g, part] + 0.1 * velocity
+                    out[c, 0, at, cells] = columns[group + g, low + 24 : low + 28] + 0.1 * velocity
 
 
 VMEM = pl.BlockSpec(memory_space=pltpu.VMEM)
 SMEM = pl.BlockSpec(memory_space=pltpu.SMEM)
+ALONE = pltpu.CompilerParams(vmem_limit_bytes=60 * 1024 * 1024)
 PARAMS = pltpu.CompilerParams(vmem_limit_bytes=40 * 1024 * 1024)
 
 
@@ -304,30 +327,48 @@
     planes, rows, cells = damage.shape
     f32 = jnp.float32
     shape = jax.ShapeDtypeStruct
-    group_shape = (GROUP, 24, LANES)
-    up, down, edge, edge_up, edge_down, first = pl.pallas_call(
-        pack_kernel,
-        out_shape=[
-            shape((8, rows, cells), f32),
-            shape((6, rows, cells), f32),
-            shape((6, 2 * planes, cells), f32),
-            shape((8, cells), f32),
-            shape((8, cells), f32),
-            shape(group_shape, f32),
-        ],
-        in_specs=[VMEM] * 3,
-        out_specs=[VMEM] * 6,
-        compiler_params=PARAMS,
-        name="pack",
-    )(displacement, damage, broken)
-
+    group_shape = (GROUP, 48, LANES)
     slabs = lax.axis_size("slab")
     upward = [(i, i + 1) for i in range(slabs - 1)]
     downward = [(i + 1, i) for i in range(slabs - 1)]
     across_up = [(2 * s + c, 2 * t + 1 - c) for s, t in upward for c in range(2)]
     across_down = [(2 * s + c, 2 * t + 1 - c) for s, t in downward for c in range(2)]
     both = ("slab", "col")
-    up = lax.ppermute(up, "slab", upward)
+    anywhere = pl.BlockSpec(memory_space=pl.ANY)
+
+    packed = pl.pallas_call(
+        pack_up_kernel,
+        out_shape=shape((8, rows, cells), f32),
+        in_specs=[pl.BlockSpec(memory_space=pltpu.HBM)] * 3,
+        out_specs=VMEM,
+        scratch_shapes=[
+            pltpu.VMEM((3, rows, cells), jnp.int32),
+            pltpu.VMEM((rows, cells), f32),
+            pltpu.SemaphoreType.DMA((9,)),
+        ],
+        compiler_params=ALONE,
+        name="pack_up",
+    )(displacement, damage, broken)
+    up = lax.ppermute(packed, "slab", upward)
+    down, edge, edge_up, edge_down = pl.pallas_call(
+        pack_rest_kernel,
+        out_shape=[
+            shape((6, rows, cells), f32),
+            shape((6, 2 * planes, cells), f32),
+            shape((8, cells), f32),
+            shape((8, cells), f32),
+        ],
+        in_specs=[pl.BlockSpec(memory_space=pltpu.HBM)] * 3 + [anywhere],
+        out_specs=[VMEM] * 4,
+        scratch_shapes=[
+            pltpu.VMEM((3, planes, 8, cells), f32),
+            pltpu.VMEM((planes, 8, cells), f32),
+            pltpu.VMEM((2, planes, 8, cells), jnp.int32),
+            pltpu.SemaphoreType.DMA((9,)),
+        ],
+        compiler_params=ALONE,
+        name="pack_rest",
+    )(displacement, damage, broken, packed)
     edge_up = lax.ppermute(edge_up, both, across_up)
     edge = lax.ppermute(edge, "col", [(0, 1), (1, 0)])
     down = lax.ppermute(down, "slab", downward)
@@ -339,46 +380,57 @@
     partner = jnp.bitwise_xor(member[None, :], jnp.left_shift(jnp.int32(1), bits)[:, None])
     taken = jnp.minimum(mine, jnp.take_along_axis(mine, partner, axis=1)).reshape(-1)
 
-    def forces(targets, out):
-        kept = len(targets) + 2
+    def forces(name, targets, low, high, out, **operands):
+        slots = sum(low <= p < high for p in range(min(targets) - 1, max(targets) + 2))
         return pl.pallas_call(
-            functools.partial(force_kernel, targets),
+            functools.partial(force_kernel, targets, low, high, tuple(operands)),
             out_shape=out,
-            in_specs=[VMEM] * 9,
+            in_specs=[anywhere if key.startswith("order") else VMEM for key in operands],
             out_specs=VMEM,
             scratch_shapes=[
-                pltpu.VMEM((4, 5, kept, 2, rows + 2 * TOP, LANES), f32),
-                pltpu.VMEM((2, 5, kept, 2, rows + 2 * TOP, LANES), jnp.int32),
+                pltpu.VMEM((4, 5, slots, 2, rows + 2 * TOP, LANES), f32),
+                pltpu.VMEM((2, 5, slots, 2, rows + 2 * TOP, LANES), jnp.int32),
             ],
             compiler_params=PARAMS,
-            name="force_first" if targets == (0,) else "force_rest",
-        )(displacement, velocity, damage, broken, up, down, edge, edge_up, edge_down)
-
-    def route(data):
-        return pl.pallas_call(
-            route_kernel,
-            out_shape=shape(group_shape, f32),
-            in_specs=[SMEM, SMEM, VMEM],
-            out_specs=VMEM,
-            scratch_shapes=[pltpu.VMEM((2,) + group_shape, f32)],
-            compiler_params=PARAMS,
-            name="route",
-        )(taken, bits, data)
-
-    second = forces((0,), shape(group_shape, f32))
-    whole = forces(tuple(range(1, planes)), shape((6, planes, rows, cells), f32))
-    first = exchange(route(exchange(first)))
-    second = exchange(route(exchange(second)))
+            name=name,
+        )(*operands.values())
+
+    own = dict(disp=displacement, damage=damage)
+    begun = forces(
+        "force_own", (0,), 0, planes, shape((3, 1, rows, cells), f32),
+        vel=velocity, broken=broken, edge=edge, **own,
+    )
+    send = forces(
+        "force_below", (0,), -2, 0, shape(group_shape, f32),
+        vel=begun, up=up, edge_up=edge_up, order=down, order_edge=edge_down, **own,
+    )
+    columns = exchange(send)
+
+    whole = forces(
+        "force_rest", tuple(range(1, planes)), -2, planes + 2, shape((6, planes, rows, cells), f32),
+        vel=velocity, broken=broken, up=up, down=down, edge=edge, edge_up=edge_up,
+        edge_down=edge_down, **own,
+    )
+    columns = pl.pallas_call(
+        route_kernel,
+        out_shape=shape(group_shape, f32),
+        in_specs=[SMEM, SMEM, VMEM],
+        out_specs=VMEM,
+        scratch_shapes=[pltpu.VMEM((2,) + group_shape, f32)],
+        compiler_params=PARAMS,
+        name="route",
+    )(taken, bits, columns)
+    columns = exchange(columns)
     return pl.pallas_call(
         place_kernel,
         out_shape=shape((6, planes, rows, cells), f32),
-        in_specs=[pl.BlockSpec(memory_space=pl.ANY)] + [pl.BlockSpec(group_shape, lambda i: (0, 0, 0))] * 2,
+        in_specs=[anywhere, pl.BlockSpec(group_shape, lambda i: (0, 0, 0))],
         out_specs=pl.BlockSpec((6, 1, rows, cells), lambda i: (0, 0, 0, 0)),
         grid=(1,),
         input_output_aliases={0: 0},
         compiler_params=PARAMS,
         name="place",
-    )(whole, first, second)
+    )(whole, columns)
 
 
 def solution(mesh):

time: 120 us -> 99.6 us (0.83)
  starting transfers between devices: 55 us -> 38.2 us
  local copies, waits for them, and re-layouts: 7.91 us -> 2.72 us
  Pallas kernels: 15.9 us -> 18.1 us
    all_to_all x4 -> x2, starting transfers between devices: 33.2 us -> 10.7 us  [exchange(): return lax.all_to_all(block, 'slab', 0, 0, axis_index_groups=groups)]
    ppermute x1, starting transfers between devices: 6.24 us -> 11.9 us  [on_device(): down = lax.ppermute(down, 'slab', downward)]
    unnamed x28 -> x16, local copies, waits for them, and re-layouts: 6.7 us -> 1.51 us
    all_to_all x4 -> x2, waiting for transfers between devices: 35.6 us -> 39.6 us  [exchange(): return lax.all_to_all(block, 'slab', 0, 0, axis_index_groups=groups)]
    ppermute x1, waiting for transfers between devices: 3.08 us -> 0.01 us  [on_device(): edge_up = lax.ppermute(edge_up, both, across_up)]
    pallas_call x5 -> x6, Pallas kernels: 14.2 us -> 16.3 us  [the longest x3 11 us: forces(): pl.pallas_call(functools.partial(force_kernel, targets, low, high, tuple(...]
  transfers between devices with their start and end apart: 9 -> 7, of which waited for: 5 -> 2; matrix products, arithmetic and copies ran while one was open for 2% -> 1% of each run, Pallas kernels for 11% -> 12%
where the time goes in v2:
time: 99.6 us; the launch traced here: 99 us
  waiting for transfers between devices  39.6 us (40%)
  starting transfers between devices  38.2 us (38%)
  Pallas kernels  18.1 us (18%)
  local copies, waits for them, and re-layouts  2.72 us (3%)
    all_to_all x2, waiting for transfers between devices, exchange(): return lax.all_to_all(block, 'slab', 0, 0, axis_index_groups=groups)  39.6 us
    ppermute x1, starting transfers between devices, on_device(): down = lax.ppermute(down, 'slab', downward)  11.9 us
    pallas_call x3, Pallas kernels, forces(): pl.pallas_call(functools.partial(force_kernel, targets, low, high, tuple(...  11 us
    all_to_all x2, starting transfers between devices, exchange(): return lax.all_to_all(block, 'slab', 0, 0, axis_index_groups=groups)  10.7 us
    ppermute x1, starting transfers between devices, on_device(): edge_down = lax.ppermute(edge_down, both, across_down)  7.86 us
    ppermute x1, starting transfers between devices, on_device(): up = lax.ppermute(packed, 'slab', upward)  3.96 us
    pallas_call x1, Pallas kernels, on_device(): pl.pallas_call(pack_up_kernel, out_shape=shape((8, rows, cells), f32), in...  2.05 us
  transfers between devices with their start and end apart: 7, of which 2 were waited for; matrix products, arithmetic and copies ran while one was open for 1% of the time, Pallas kernels for 12%

profile of v2, /device:TPU:24, one launch (start us, length us, event | category | flops | bytes accessed | tf_op | source)
XLA Modules:
  0.0 99.0 jit_solution(254979443399069166)
XLA Ops:
  0.0 2.1 %pack_up.1.order = f32[8,64,256]{2,1,0:T(8,128)} custom-call(f32[3,4,64,256]{3,2,1,0:T(8,128)} %refs_5_.1, f32[4,64,256]{2,1,0:T(8,128)} %refs_6_.1, s32[2,4,64,256]{3,2,1,0:T(8,128)} %refs_1_.3), custom_call_target="tpu_custom_call" | custom-call | tf_op jit(solution)/shard_map/pack_up/pallas_call | solution.py:339
  2.1 0.0 copy-start
  2.1 0.0 copy-start.1
  2.1 0.0 copy-start.2
  2.1 4.0 %collective-permute-start = (f32[8,64,256]{2,1,0:T(8,128)}, f32[8,64,256]{2,1,0:T(8,128)S(1)}, u32[]{:S(2)}, u32[]{:S(2)}) collective-permute-start(f32[8,64,256]{2,1,0:T(8,128)} %pack_up.1.order), channel_id=1, source_target_pairs={{0,2},{2,4},{4,6},{6,8},{8,10},{10,12},{12,14},{14,16},{16,18},{18... | collective-permute-start | bytes 1572872 | tf_op jit(solution)/shard_map/ppermute | solution.py:352
  6.1 2.0 %pack_rest.1 = (f32[6,64,256]{2,1,0:T(8,128)}, f32[6,8,256]{2,1,0:T(8,128)}, f32[8,256]{1,0:T(8,128)}, f32[8,256]{1,0:T(8,128)}) custom-call(f32[3,4,64,256]{3,2,1,0:T(8,128)} %refs_5_.1, f32[4,64,256]{2,1,0:T(8,128)} %refs_6_.1, s32[2,4,64,256]{3,2,1,0:T(8,128)} %refs_1_.3, f32[8,64,256]{2,1,0:T(8,128)} %pack_up.1.order), custom_call_target="tpu_custom_call" | custom-call | tf_op jit(solution)/shard_map/pack_rest/pallas_call | solution.py:353
  8.1 11.9 %collective-permute-start.1 = (f32[6,64,256]{2,1,0:T(8,128)}, f32[6,64,256]{2,1,0:T(8,128)S(1)}, u32[]{:S(2)}, u32[]{:S(2)}) collective-permute-start(f32[6,64,256]{2,1,0:T(8,128)} %get-tuple-element.9), channel_id=1, source_target_pairs={{2,0},{4,2},{6,4},{8,6},{10,8},{12,10},{14,12},{16,14},{18,16},{20... | collective-permute-start | bytes 1179656 | tf_op jit(solution)/shard_map/ppermute | solution.py:374
  19.9 1.9 %collective-permute-start.2 = (f32[6,8,256]{2,1,0:T(8,128)}, f32[6,8,256]{2,1,0:T(8,128)S(1)}, u32[]{:S(2)}, u32[]{:S(2)}) collective-permute-start(f32[6,8,256]{2,1,0:T(8,128)} %get-tuple-element.10), channel_id=1, source_target_pairs={{0,1},{1,0},{2,3},{3,2},{4,5},{5,4},{6,7},{7,6},{8,9},{9,8},{10,11... | collective-permute-start | bytes 147464 | tf_op jit(solution)/shard_map/ppermute | solution.py:373
  21.9 1.9 %collective-permute-start.3 = (f32[8,256]{1,0:T(8,128)}, f32[8,256]{1,0:T(8,128)S(1)}, u32[]{:S(2)}, u32[]{:S(2)}) collective-permute-start(f32[8,256]{1,0:T(8,128)} %get-tuple-element.11), channel_id=1, source_target_pairs={{0,3},{1,2},{2,5},{3,4},{4,7},{5,6},{6,9},{7,8},{8,11},{9,10},{10,... | collective-permute-start | bytes 24584 | tf_op jit(solution)/shard_map/ppermute | solution.py:372
  23.8 7.9 %collective-permute-start.4 = (f32[8,256]{1,0:T(8,128)}, f32[8,256]{1,0:T(8,128)S(1)}, u32[]{:S(2)}, u32[]{:S(2)}) collective-permute-start(f32[8,256]{1,0:T(8,128)} %get-tuple-element.12), channel_id=1, source_target_pairs={{2,1},{3,0},{4,3},{5,2},{6,5},{7,4},{8,7},{9,6},{10,9},{11,8},{12,... | collective-permute-start | bytes 24584 | tf_op jit(solution)/shard_map/ppermute | solution.py:375
  31.7 0.0 collective-permute-done.2.refs_4_.refs_2_
  31.7 2.2 %force_own.1.refs_0_ = f32[3,1,64,256]{3,2,1,0:T(8,128)S(1)} custom-call(f32[3,4,64,256]{3,2,1,0:T(8,128)S(1)} %copy-done.3, s32[2,4,64,256]{3,2,1,0:T(8,128)S(1)} %copy-done.1, f32[6,8,256]{2,1,0:T(8,128)S(1)} %collective-permute-done.2.refs_4_.refs_2_, f32[3,4,64,256]{3,2,1,0:T(8,128)S(1)} %copy-done, f32[4,64,256]{2,1,0:T(8,128)S(1)} %copy-done.2), custom_call_target="tpu_custom_call" | custom-call | tf_op jit(solution)/shard_map/force_own/pallas_call | solution.py:385
  33.9 0.0 copy-start.6
  34.0 0.0 copy-start.7
  34.0 1.2 %force_below.1 = f32[16,48,128]{2,1,0:T(8,128)S(1)} custom-call(f32[3,1,64,256]{3,2,1,0:T(8,128)S(1)} %force_own.1.refs_0_, f32[8,64,256]{2,1,0:T(8,128)S(1)} %collective-permute-done.refs_2_.refs_1_, f32[8,256]{1,0:T(8,128)S(1)} %collective-permute-done.3.refs_5_.refs_2_, f32[6,64,256]{2,1,0:T(8,128)S(1)} %collective-permute-done.1.refs_3_, ...), custom_call_target="tpu_custom_call" | custom-call | tf_op jit(solution)/shard_map/force_below/pallas_call | solution.py:385
  35.2 0.0 copy-start.4
  35.2 0.7 copy-done.4
  35.9 4.2 %all-to-all-start = ((f32[16,48,128]{2,1,0:T(8,128)}), f32[16,48,128]{2,1,0:T(8,128)}, u32[]{:S(2)}, u32[]{:S(2)}) async-start(f32[16,48,128]{2,1,0:T(8,128)} %copy-done.4), calls=%async_computation | async-start | bytes 786432 | tf_op jit(solution)/shard_map/all_to_all | solution.py:323
  40.2 0.1 fusion.2
  40.3 0.1 reshape.62
  40.4 0.1 dynamic-slice_bitcast_fusion
  40.4 0.9 gather_fusion
  41.3 0.1 reshape.65
  41.4 0.1 select_minimum_fusion
  41.5 0.1 reshape.61.taken
  41.6 23.0 %all-to-all-done.data = f32[16,48,128]{2,1,0:T(8,128)} async-done(((f32[16,48,128]{2,1,0:T(8,128)}), f32[16,48,128]{2,1,0:T(8,128)}, u32[]{:S(2)}, u32[]{:S(2)}) %all-to-all-start) | async-done | bytes 393248 | tf_op jit(solution)/shard_map/all_to_all | solution.py:323
  64.5 1.2 %route.1 = f32[16,48,128]{2,1,0:T(8,128)S(1)} custom-call(s32[64]{0:T(128)S(1)} %reshape.61.taken, s32[4]{0:T(128)S(1)} %copy-done.6, f32[16,48,128]{2,1,0:T(8,128)} %all-to-all-done.data), custom_call_target="tpu_custom_call" | custom-call | tf_op jit(solution)/shard_map/route/pallas_call | solution.py:414
  65.7 0.7 copy-done.5
  66.5 6.4 %all-to-all-start.1 = ((f32[16,48,128]{2,1,0:T(8,128)}), f32[16,48,128]{2,1,0:T(8,128)}, u32[]{:S(2)}, u32[]{:S(2)}) async-start(f32[16,48,128]{2,1,0:T(8,128)} %copy-done.5), calls=%async_computation.1 | async-start | bytes 786432 | tf_op jit(solution)/shard_map/all_to_all | solution.py:323
  72.9 7.6 %force_rest.1.whole = f32[6,4,64,256]{3,2,1,0:T(8,128)} custom-call(f32[3,4,64,256]{3,2,1,0:T(8,128)S(1)} %copy-done.3, s32[2,4,64,256]{3,2,1,0:T(8,128)S(1)} %copy-done.1, f32[8,64,256]{2,1,0:T(8,128)S(1)} %collective-permute-done.refs_2_.refs_1_, f32[6,64,256]{2,1,0:T(8,128)S(1)} %collective-permute-done.1.refs_3_, ...), custom_call_target="tpu_custom_call" | custom-call | tf_op jit(solution)/shard_map/force_rest/pallas_call | solution.py:385
  80.6 16.6 %all-to-all-done.1.columns = f32[16,48,128]{2,1,0:T(8,128)} async-done(((f32[16,48,128]{2,1,0:T(8,128)}), f32[16,48,128]{2,1,0:T(8,128)}, u32[]{:S(2)}, u32[]{:S(2)}) %all-to-all-start.1) | async-done | bytes 393248 | tf_op jit(solution)/shard_map/all_to_all | solution.py:323
  97.2 1.8 %place.1 = f32[6,4,64,256]{3,2,1,0:T(8,128)} custom-call(f32[6,4,64,256]{3,2,1,0:T(8,128)} %force_rest.1.whole, f32[16,48,128]{2,1,0:T(8,128)} %all-to-all-done.1.columns), custom_call_target="tpu_custom_call", output_to_operand_aliasing={{}: (0, {})} | custom-call | tf_op jit(solution)/shard_map/place/pallas_call | solution.py:424
  (13 shorter events, 0.0 us)
Async XLA Ops:
  0.0 31.7 %copy-start.3 = (f32[3,4,64,256]{3,2,1,0:T(8,128)S(1)}, f32[3,4,64,256]{3,2,1,0:T(8,128)}, u32[]{:S(2)}) copy-start(f32[3,4,64,256]{3,2,1,0:T(8,128)} %refs_0_.3) | copy-start | bytes 2359300
  2.1 29.6 %copy-start = (f32[3,4,64,256]{3,2,1,0:T(8,128)S(1)}, f32[3,4,64,256]{3,2,1,0:T(8,128)}, u32[]{:S(2)}) copy-start(f32[3,4,64,256]{3,2,1,0:T(8,128)} %refs_5_.1) | copy-start | bytes 2359300
  2.1 29.6 %copy-start.1 = (s32[2,4,64,256]{3,2,1,0:T(8,128)S(1)}, s32[2,4,64,256]{3,2,1,0:T(8,128)}, u32[]{:S(2)}) copy-start(s32[2,4,64,256]{3,2,1,0:T(8,128)} %refs_1_.3) | copy-start | bytes 1572868
  2.1 29.6 %copy-start.2 = (f32[4,64,256]{2,1,0:T(8,128)S(1)}, f32[4,64,256]{2,1,0:T(8,128)}, u32[]{:S(2)}) copy-start(f32[4,64,256]{2,1,0:T(8,128)} %refs_6_.1) | copy-start | bytes 786436
  2.1 31.9 %collective-permute-start = (f32[8,64,256]{2,1,0:T(8,128)}, f32[8,64,256]{2,1,0:T(8,128)S(1)}, u32[]{:S(2)}, u32[]{:S(2)}) collective-permute-start(f32[8,64,256]{2,1,0:T(8,128)} %pack_up.1.order), channel_id=1, source_target_pairs={{0,2},{2,4},{4,6},{6,8},{8,10},{10,12},{12,14},{14,16},{16,18},{18... | collective-permute-start | bytes 1572872 | tf_op jit(solution)/shard_map/ppermute | solution.py:352
  8.1 25.9 %collective-permute-start.1 = (f32[6,64,256]{2,1,0:T(8,128)}, f32[6,64,256]{2,1,0:T(8,128)S(1)}, u32[]{:S(2)}, u32[]{:S(2)}) collective-permute-start(f32[6,64,256]{2,1,0:T(8,128)} %get-tuple-element.9), channel_id=1, source_target_pairs={{2,0},{4,2},{6,4},{8,6},{10,8},{12,10},{14,12},{16,14},{18,16},{20... | collective-permute-start | bytes 1179656 | tf_op jit(solution)/shard_map/ppermute | solution.py:374
  19.9 11.7 %collective-permute-start.2 = (f32[6,8,256]{2,1,0:T(8,128)}, f32[6,8,256]{2,1,0:T(8,128)S(1)}, u32[]{:S(2)}, u32[]{:S(2)}) collective-permute-start(f32[6,8,256]{2,1,0:T(8,128)} %get-tuple-element.10), channel_id=1, source_target_pairs={{0,1},{1,0},{2,3},{3,2},{4,5},{5,4},{6,7},{7,6},{8,9},{9,8},{10,11... | collective-permute-start | bytes 147464 | tf_op jit(solution)/shard_map/ppermute | solution.py:373
  21.9 12.1 %collective-permute-start.3 = (f32[8,256]{1,0:T(8,128)}, f32[8,256]{1,0:T(8,128)S(1)}, u32[]{:S(2)}, u32[]{:S(2)}) collective-permute-start(f32[8,256]{1,0:T(8,128)} %get-tuple-element.11), channel_id=1, source_target_pairs={{0,3},{1,2},{2,5},{3,4},{4,7},{5,6},{6,9},{7,8},{8,11},{9,10},{10,... | collective-permute-start | bytes 24584 | tf_op jit(solution)/shard_map/ppermute | solution.py:372
  23.8 10.2 %collective-permute-start.4 = (f32[8,256]{1,0:T(8,128)}, f32[8,256]{1,0:T(8,128)S(1)}, u32[]{:S(2)}, u32[]{:S(2)}) collective-permute-start(f32[8,256]{1,0:T(8,128)} %get-tuple-element.12), channel_id=1, source_target_pairs={{2,1},{3,0},{4,3},{5,2},{6,5},{7,4},{8,7},{9,6},{10,9},{11,8},{12,... | collective-permute-start | bytes 24584 | tf_op jit(solution)/shard_map/ppermute | solution.py:375
  33.9 6.2 %copy-start.6 = (s32[4]{0:T(128)S(1)}, s32[4]{0:T(128)}, u32[]{:S(2)}) copy-start(s32[4]{0:T(128)} %bits.1) | copy-start | bytes 52
  34.0 6.4 %copy-start.7 = (s32[256,4]{0,1:T(4,128)S(1)}, s32[256,4]{0,1:T(4,128)}, u32[]{:S(2)}) copy-start(s32[256,4]{0,1:T(4,128)} %param.10) | copy-start | bytes 12292
  35.2 0.7 copy-start.4
  35.9 28.6 %all-to-all-start = ((f32[16,48,128]{2,1,0:T(8,128)}), f32[16,48,128]{2,1,0:T(8,128)}, u32[]{:S(2)}, u32[]{:S(2)}) async-start(f32[16,48,128]{2,1,0:T(8,128)} %copy-done.4), calls=%async_computation | async-start | bytes 786432 | tf_op jit(solution)/shard_map/all_to_all | solution.py:323
  65.7 0.7 copy-start.5
  66.5 30.7 %all-to-all-start.1 = ((f32[16,48,128]{2,1,0:T(8,128)}), f32[16,48,128]{2,1,0:T(8,128)}, u32[]{:S(2)}, u32[]{:S(2)}) async-start(f32[16,48,128]{2,1,0:T(8,128)} %copy-done.5), calls=%async_computation.1 | async-start | bytes 786432 | tf_op jit(solution)/shard_map/all_to_all | solution.py:323

commit v3 on v2

--- a/solution.py
+++ b/solution.py
@@ -39,29 +39,10 @@
     return (flags & (1 << (index % 8))) == 0
 
 
-def pack_up_kernel(disp, damage, broken, up, words, scale, sems):
-    last = damage.shape[0] - 1
-    moves = [(disp.at[c, last], up.at[c]) for c in range(3)]
-    moves += [(damage.at[last], up.at[3]), (disp.at[0, last - 1], up.at[6])]
-    moves += [(broken.at[w, last], words.at[w]) for w in range(2)]
-    moves += [(broken.at[1, last - 1], words.at[2]), (damage.at[last - 1], scale)]
-    copies = [
-        pltpu.make_async_copy(source, target, sems.at[i])
-        for i, (source, target) in enumerate(moves)
-    ]
-    for copy in copies:
-        copy.start()
-    for copy in copies:
-        copy.wait()
-    up[4] = words[0].astype(jnp.float32)
-    up[5] = words[1].astype(jnp.float32)
-    up[7] = jnp.where(alive_of(words[2], 15), scale[...], 0.0)
-
-
-def pack_rest_kernel(
-    disp, damage, broken, order, down, edge, edge_up, edge_down, disp_rim, damage_rim, words, sems
+def pack_kernel(
+    disp, damage, broken, up, down, edge, edge_up, edge_down, disp_rim, damage_rim, words, flags,
+    scale, sems
 ):
-    del order
     position = lax.axis_index("col")
     planes, rows = damage.shape[0], damage.shape[1]
     last = planes - 1
@@ -75,6 +56,10 @@
         (damage.at[1], down.at[5]),
     ]
     moves += [(disp.at[c, 0], down.at[c]) for c in range(3)]
+    moves += [(disp.at[c, last], up.at[c]) for c in range(3)]
+    moves += [(damage.at[last], up.at[3]), (disp.at[0, last - 1], up.at[6])]
+    moves += [(broken.at[w, last], flags.at[w]) for w in range(2)]
+    moves += [(broken.at[1, last - 1], flags.at[2]), (damage.at[last - 1], scale)]
     copies = [
         pltpu.make_async_copy(source, target, sems.at[i])
         for i, (source, target) in enumerate(moves)
@@ -85,6 +70,9 @@
     edge_down[...] = jnp.zeros(edge_down.shape, jnp.float32)
     for copy in copies:
         copy.wait()
+    up[4] = flags[0].astype(jnp.float32)
+    up[5] = flags[1].astype(jnp.float32)
+    up[7] = jnp.where(alive_of(flags[2], 15), scale[...], 0.0)
 
     def edges(first, inner):
         for plane in range(planes):
@@ -281,7 +269,8 @@
     lax.fori_loop(0, rows // 8, block, 0)
 
 
-def route_kernel(taken, bits, data, out, scratch):
+def route_kernel(taken, bits, data, order, out, scratch):
+    del order
     member = lax.rem(lax.axis_index("slab"), GROUP)
     column = 4 * member + lax.rem(lax.broadcasted_iota(jnp.int32, (48, LANES), 0), 4)
     for turn in range(4):
@@ -336,43 +325,32 @@
     both = ("slab", "col")
     anywhere = pl.BlockSpec(memory_space=pl.ANY)
 
-    packed = pl.pallas_call(
-        pack_up_kernel,
-        out_shape=shape((8, rows, cells), f32),
-        in_specs=[pl.BlockSpec(memory_space=pltpu.HBM)] * 3,
-        out_specs=VMEM,
-        scratch_shapes=[
-            pltpu.VMEM((3, rows, cells), jnp.int32),
-            pltpu.VMEM((rows, cells), f32),
-            pltpu.SemaphoreType.DMA((9,)),
-        ],
-        compiler_params=ALONE,
-        name="pack_up",
-    )(displacement, damage, broken)
-    up = lax.ppermute(packed, "slab", upward)
-    down, edge, edge_up, edge_down = pl.pallas_call(
-        pack_rest_kernel,
+    up, down, edge, edge_up, edge_down = pl.pallas_call(
+        pack_kernel,
         out_shape=[
+            shape((8, rows, cells), f32),
             shape((6, rows, cells), f32),
             shape((6, 2 * planes, cells), f32),
             shape((8, cells), f32),
             shape((8, cells), f32),
         ],
-        in_specs=[pl.BlockSpec(memory_space=pltpu.HBM)] * 3 + [anywhere],
-        out_specs=[VMEM] * 4,
+        in_specs=[pl.BlockSpec(memory_space=pltpu.HBM)] * 3,
+        out_specs=[VMEM] * 5,
         scratch_shapes=[
             pltpu.VMEM((3, planes, 8, cells), f32),
             pltpu.VMEM((planes, 8, cells), f32),
             pltpu.VMEM((2, planes, 8, cells), jnp.int32),
-            pltpu.SemaphoreType.DMA((9,)),
+            pltpu.VMEM((3, rows, cells), jnp.int32),
+            pltpu.VMEM((rows, cells), f32),
+            pltpu.SemaphoreType.DMA((18,)),
         ],
         compiler_params=ALONE,
-        name="pack_rest",
-    )(displacement, damage, broken, packed)
+        name="pack",
+    )(displacement, damage, broken)
+    up = lax.ppermute(up, "slab", upward)
     edge_up = lax.ppermute(edge_up, both, across_up)
     edge = lax.ppermute(edge, "col", [(0, 1), (1, 0)])
     down = lax.ppermute(down, "slab", downward)
-    edge_down = lax.ppermute(edge_down, both, across_down)
 
     member = jnp.arange(GROUP, dtype=jnp.int32)
     base = lax.axis_index("slab") // GROUP * GROUP
@@ -402,9 +380,11 @@
     )
     send = forces(
         "force_below", (0,), -2, 0, shape(group_shape, f32),
-        vel=begun, up=up, edge_up=edge_up, order=down, order_edge=edge_down, **own,
+        vel=begun, up=up, edge_up=edge_up, order=down, **own,
     )
+    edge_down, send = lax.optimization_barrier((edge_down, send))
     columns = exchange(send)
+    edge_down = lax.ppermute(edge_down, both, across_down)
 
     whole = forces(
         "force_rest", tuple(range(1, planes)), -2, planes + 2, shape((6, planes, rows, cells), f32),
@@ -414,12 +394,12 @@
     columns = pl.pallas_call(
         route_kernel,
         out_shape=shape(group_shape, f32),
-        in_specs=[SMEM, SMEM, VMEM],
+        in_specs=[SMEM, SMEM, VMEM, anywhere],
         out_specs=VMEM,
         scratch_shapes=[pltpu.VMEM((2,) + group_shape, f32)],
         compiler_params=PARAMS,
         name="route",
-    )(taken, bits, columns)
+    )(taken, bits, columns, edge_down)
     columns = exchange(columns)
     return pl.pallas_call(
         place_kernel,

time: 99.6 us -> 95.9 us (0.963)
  waiting for transfers between devices: 39.6 us -> 37.2 us
    all_to_all x2, waiting for transfers between devices: 39.6 us -> 25.6 us  [exchange(): return lax.all_to_all(block, 'slab', 0, 0, axis_index_groups=groups)]
    ppermute x1, waiting for transfers between devices: 0.01 us -> 7.53 us  [on_device(): edge_down = lax.ppermute(edge_down, both, across_down)]
    ppermute x1, waiting for transfers between devices: 0.01 us -> 4.05 us  [on_device(): edge_up = lax.ppermute(edge_up, both, across_up)]
    pallas_call x2 -> x1, Pallas kernels: 4.04 us -> 2.53 us  [on_device(): pl.pallas_call(pack_kernel, out_shape=[shape((8, rows, cells), f32), shap...]
    ppermute x1, starting transfers between devices: 7.86 us -> 6.55 us  [on_device(): edge_down = lax.ppermute(edge_down, both, across_down)]
  transfers between devices with their start and end apart: 7 -> 7, of which waited for: 2 -> 4; matrix products, arithmetic and copies ran while one was open for 1% -> 1% of each run, Pallas kernels for 12% -> 10%
where the time goes in v3:
time: 95.9 us; the launch traced here: 95.3 us
  starting transfers between devices  37.4 us (39%)
  waiting for transfers between devices  37.2 us (39%)
  Pallas kernels  17.3 us (18%)
  local copies, waits for them, and re-layouts  3.11 us (3%)
    all_to_all x2, waiting for transfers between devices, exchange(): return lax.all_to_all(block, 'slab', 0, 0, axis_index_groups=groups)  25.6 us
    ppermute x1, starting transfers between devices, on_device(): down = lax.ppermute(down, 'slab', downward)  11.9 us
    pallas_call x3, Pallas kernels, forces(): pl.pallas_call(functools.partial(force_kernel, targets, low, high, tuple(...  11.8 us
    all_to_all x2, starting transfers between devices, exchange(): return lax.all_to_all(block, 'slab', 0, 0, axis_index_groups=groups)  11.3 us
    ppermute x1, waiting for transfers between devices, on_device(): edge_down = lax.ppermute(edge_down, both, across_down)  7.53 us
    ppermute x1, starting transfers between devices, on_device(): edge_down = lax.ppermute(edge_down, both, across_down)  6.55 us
    ppermute x1, waiting for transfers between devices, on_device(): edge_up = lax.ppermute(edge_up, both, across_up)  4.05 us
    ppermute x1, starting transfers between devices, on_device(): up = lax.ppermute(up, 'slab', upward)  3.83 us
  transfers between devices with their start and end apart: 7, of which 4 were waited for; matrix products, arithmetic and copies ran while one was open for 1% of the time, Pallas kernels for 10%

profile of v3, /device:TPU:24, one launch (start us, length us, event | category | flops | bytes accessed | tf_op | source)
XLA Modules:
  0.0 95.3 jit_solution(7649155095908536276)
XLA Ops:
  0.0 2.5 %pack.1 = (f32[8,64,256]{2,1,0:T(8,128)}, f32[6,64,256]{2,1,0:T(8,128)}, f32[6,8,256]{2,1,0:T(8,128)}, f32[8,256]{1,0:T(8,128)}, f32[8,256]{1,0:T(8,128)}) custom-call(f32[3,4,64,256]{3,2,1,0:T(8,128)} %refs_7_.1, f32[4,64,256]{2,1,0:T(8,128)} %refs_8_.1, s32[2,4,64,256]{3,2,1,0:T(8,128)} %refs_1_.3), custom_call_target="tpu_custom_call" | custom-call | tf_op jit(solution)/shard_map/pack/pallas_call | solution.py:328
  2.5 3.8 %collective-permute-start = (f32[8,64,256]{2,1,0:T(8,128)}, f32[8,64,256]{2,1,0:T(8,128)S(1)}, u32[]{:S(2)}, u32[]{:S(2)}) collective-permute-start(f32[8,64,256]{2,1,0:T(8,128)} %get-tuple-element.12), channel_id=1, source_target_pairs={{0,2},{2,4},{4,6},{6,8},{8,10},{10,12},{12,14},{14,16},{16,18},{18... | collective-permute-start | bytes 1572872 | tf_op jit(solution)/shard_map/ppermute | solution.py:350
  6.4 11.9 %collective-permute-start.1 = (f32[6,64,256]{2,1,0:T(8,128)}, f32[6,64,256]{2,1,0:T(8,128)S(1)}, u32[]{:S(2)}, u32[]{:S(2)}) collective-permute-start(f32[6,64,256]{2,1,0:T(8,128)} %get-tuple-element.13), channel_id=1, source_target_pairs={{2,0},{4,2},{6,4},{8,6},{10,8},{12,10},{14,12},{16,14},{18,16},{20... | collective-permute-start | bytes 1179656 | tf_op jit(solution)/shard_map/ppermute | solution.py:353
  18.3 1.9 %collective-permute-start.2 = (f32[6,8,256]{2,1,0:T(8,128)}, f32[6,8,256]{2,1,0:T(8,128)S(1)}, u32[]{:S(2)}, u32[]{:S(2)}) collective-permute-start(f32[6,8,256]{2,1,0:T(8,128)} %get-tuple-element.14), channel_id=1, source_target_pairs={{0,1},{1,0},{2,3},{3,2},{4,5},{5,4},{6,7},{7,6},{8,9},{9,8},{10,11... | collective-permute-start | bytes 147464 | tf_op jit(solution)/shard_map/ppermute | solution.py:352
  20.2 1.9 %collective-permute-start.3 = (f32[8,256]{1,0:T(8,128)}, f32[8,256]{1,0:T(8,128)S(1)}, u32[]{:S(2)}, u32[]{:S(2)}) collective-permute-start(f32[8,256]{1,0:T(8,128)} %get-tuple-element.15), channel_id=1, source_target_pairs={{0,3},{1,2},{2,5},{3,4},{4,7},{5,6},{6,9},{7,8},{8,11},{9,10},{10,... | collective-permute-start | bytes 24584 | tf_op jit(solution)/shard_map/ppermute | solution.py:351
  22.1 0.0 collective-permute-done.2.refs_2_.refs_4_
  22.2 0.0 copy-start.3
  22.2 1.1 %copy-done.3 = f32[3,4,64,256]{3,2,1,0:T(8,128)S(1)} copy-done((f32[3,4,64,256]{3,2,1,0:T(8,128)S(1)}, f32[3,4,64,256]{3,2,1,0:T(8,128)}, u32[]{:S(2)}) %copy-start.3) | copy-done | bytes 786456
  23.3 2.2 %force_own.1.refs_0_ = f32[3,1,64,256]{3,2,1,0:T(8,128)S(1)} custom-call(f32[3,4,64,256]{3,2,1,0:T(8,128)S(1)} %copy-done.3, s32[2,4,64,256]{3,2,1,0:T(8,128)S(1)} %copy-done.1, f32[6,8,256]{2,1,0:T(8,128)S(1)} %collective-permute-done.2.refs_2_.refs_4_, f32[3,4,64,256]{3,2,1,0:T(8,128)S(1)} %copy-done, f32[4,64,256]{2,1,0:T(8,128)S(1)} %copy-done.2), custom_call_target="tpu_custom_call" | custom-call | tf_op jit(solution)/shard_map/force_own/pallas_call | solution.py:363
  25.5 0.0 copy-start.6
  25.5 0.0 copy-start.7
  25.5 4.1 %collective-permute-done.3.refs_2_.refs_5_ = f32[8,256]{1,0:T(8,128)S(1)} collective-permute-done((f32[8,256]{1,0:T(8,128)}, f32[8,256]{1,0:T(8,128)S(1)}, u32[]{:S(2)}, u32[]{:S(2)}) %collective-permute-start.3) | collective-permute-done | bytes 8224 | tf_op jit(solution)/shard_map/ppermute | solution.py:351
  29.6 0.0 collective-permute-done.1.refs_3_
  29.6 0.0 collective-permute-done.refs_1_.refs_2_
  29.6 1.9 %force_below.1 = f32[16,48,128]{2,1,0:T(8,128)} custom-call(f32[3,1,64,256]{3,2,1,0:T(8,128)S(1)} %force_own.1.refs_0_, f32[8,64,256]{2,1,0:T(8,128)S(1)} %collective-permute-done.refs_1_.refs_2_, f32[8,256]{1,0:T(8,128)S(1)} %collective-permute-done.3.refs_2_.refs_5_, f32[6,64,256]{2,1,0:T(8,128)S(1)} %collective-permute-done.1.refs_3_, ...), custom_call_target="tpu_custom_call" | custom-call | tf_op jit(solution)/shard_map/force_below/pallas_call | solution.py:363
  31.5 5.4 %all-to-all-start = ((f32[16,48,128]{2,1,0:T(8,128)}), f32[16,48,128]{2,1,0:T(8,128)}, u32[]{:S(2)}, u32[]{:S(2)}) async-start(f32[16,48,128]{2,1,0:T(8,128)} %force_below.1), calls=%async_computation | async-start | bytes 786432 | tf_op jit(solution)/shard_map/all_to_all | solution.py:312
  36.9 0.1 fusion.2
  37.0 0.1 reshape.62
  37.1 0.1 dynamic-slice_bitcast_fusion
  37.2 0.9 gather_fusion
  38.1 0.1 reshape.65
  38.1 6.5 %collective-permute-start.4 = (f32[8,256]{1,0:T(8,128)S(1)}, f32[8,256]{1,0:T(8,128)S(1)}, u32[]{:S(2)}, u32[]{:S(2)}) collective-permute-start(f32[8,256]{1,0:T(8,128)S(1)} %copy-done.8), channel_id=1, source_target_pairs={{2,1},{3,0},{4,3},{5,2},{6,5},{7,4},{8,7},{9,6},{10,9},{11,8},{12,... | collective-permute-start | bytes 24584 | tf_op jit(solution)/shard_map/ppermute | solution.py:387
  44.7 0.1 select_minimum_fusion
  44.8 0.1 reshape.61.taken
  44.9 7.5 %collective-permute-done.4.refs_6_.order = f32[8,256]{1,0:T(8,128)S(1)} collective-permute-done((f32[8,256]{1,0:T(8,128)S(1)}, f32[8,256]{1,0:T(8,128)S(1)}, u32[]{:S(2)}, u32[]{:S(2)}) %collective-permute-start.4) | collective-permute-done | bytes 8224 | tf_op jit(solution)/shard_map/ppermute | solution.py:387
  52.4 8.9 %all-to-all-done.data = f32[16,48,128]{2,1,0:T(8,128)} async-done(((f32[16,48,128]{2,1,0:T(8,128)}), f32[16,48,128]{2,1,0:T(8,128)}, u32[]{:S(2)}, u32[]{:S(2)}) %all-to-all-start) | async-done | bytes 393248 | tf_op jit(solution)/shard_map/all_to_all | solution.py:312
  61.3 1.2 %route.1 = f32[16,48,128]{2,1,0:T(8,128)S(1)} custom-call(s32[64]{0:T(128)S(1)} %reshape.61.taken, s32[4]{0:T(128)S(1)} %copy-done.6, f32[16,48,128]{2,1,0:T(8,128)} %all-to-all-done.data, f32[8,256]{1,0:T(8,128)S(1)} %collective-permute-done.4.refs_6_.order), custom_call_target="tpu_custom_call" | custom-call | tf_op jit(solution)/shard_map/route/pallas_call | solution.py:394
  62.5 0.7 copy-done.5
  63.2 5.9 %all-to-all-start.1 = ((f32[16,48,128]{2,1,0:T(8,128)}), f32[16,48,128]{2,1,0:T(8,128)}, u32[]{:S(2)}, u32[]{:S(2)}) async-start(f32[16,48,128]{2,1,0:T(8,128)} %copy-done.5), calls=%async_computation.1 | async-start | bytes 786432 | tf_op jit(solution)/shard_map/all_to_all | solution.py:312
  69.1 7.6 %force_rest.1.whole = f32[6,4,64,256]{3,2,1,0:T(8,128)} custom-call(f32[3,4,64,256]{3,2,1,0:T(8,128)S(1)} %copy-done.4, s32[2,4,64,256]{3,2,1,0:T(8,128)S(1)} %copy-done.1, f32[8,64,256]{2,1,0:T(8,128)S(1)} %collective-permute-done.refs_1_.refs_2_, f32[6,64,256]{2,1,0:T(8,128)S(1)} %collective-permute-done.1.refs_3_, ...), custom_call_target="tpu_custom_call" | custom-call | tf_op jit(solution)/shard_map/force_rest/pallas_call | solution.py:363
  76.8 16.7 %all-to-all-done.1.columns = f32[16,48,128]{2,1,0:T(8,128)} async-done(((f32[16,48,128]{2,1,0:T(8,128)}), f32[16,48,128]{2,1,0:T(8,128)}, u32[]{:S(2)}, u32[]{:S(2)}) %all-to-all-start.1) | async-done | bytes 393248 | tf_op jit(solution)/shard_map/all_to_all | solution.py:312
  93.5 1.8 %place.1 = f32[6,4,64,256]{3,2,1,0:T(8,128)} custom-call(f32[6,4,64,256]{3,2,1,0:T(8,128)} %force_rest.1.whole, f32[16,48,128]{2,1,0:T(8,128)} %all-to-all-done.1.columns), custom_call_target="tpu_custom_call", output_to_operand_aliasing={{}: (0, {})} | custom-call | tf_op jit(solution)/shard_map/place/pallas_call | solution.py:404
  (14 shorter events, 0.0 us)
Async XLA Ops:
  0.0 22.1 %copy-start.2 = (f32[4,64,256]{2,1,0:T(8,128)S(1)}, f32[4,64,256]{2,1,0:T(8,128)}, u32[]{:S(2)}) copy-start(f32[4,64,256]{2,1,0:T(8,128)} %refs_8_.1) | copy-start | bytes 786436
  0.0 22.1 %copy-start = (f32[3,4,64,256]{3,2,1,0:T(8,128)S(1)}, f32[3,4,64,256]{3,2,1,0:T(8,128)}, u32[]{:S(2)}) copy-start(f32[3,4,64,256]{3,2,1,0:T(8,128)} %refs_7_.1) | copy-start | bytes 2359300
  0.0 22.1 %copy-start.1 = (s32[2,4,64,256]{3,2,1,0:T(8,128)S(1)}, s32[2,4,64,256]{3,2,1,0:T(8,128)}, u32[]{:S(2)}) copy-start(s32[2,4,64,256]{3,2,1,0:T(8,128)} %refs_1_.3) | copy-start | bytes 1572868
  2.5 27.0 %collective-permute-start = (f32[8,64,256]{2,1,0:T(8,128)}, f32[8,64,256]{2,1,0:T(8,128)S(1)}, u32[]{:S(2)}, u32[]{:S(2)}) collective-permute-start(f32[8,64,256]{2,1,0:T(8,128)} %get-tuple-element.12), channel_id=1, source_target_pairs={{0,2},{2,4},{4,6},{6,8},{8,10},{10,12},{12,14},{14,16},{16,18},{18... | collective-permute-start | bytes 1572872 | tf_op jit(solution)/shard_map/ppermute | solution.py:350
  6.4 23.2 %collective-permute-start.1 = (f32[6,64,256]{2,1,0:T(8,128)}, f32[6,64,256]{2,1,0:T(8,128)S(1)}, u32[]{:S(2)}, u32[]{:S(2)}) collective-permute-start(f32[6,64,256]{2,1,0:T(8,128)} %get-tuple-element.13), channel_id=1, source_target_pairs={{2,0},{4,2},{6,4},{8,6},{10,8},{12,10},{14,12},{16,14},{18,16},{20... | collective-permute-start | bytes 1179656 | tf_op jit(solution)/shard_map/ppermute | solution.py:353
  18.3 3.9 %collective-permute-start.2 = (f32[6,8,256]{2,1,0:T(8,128)}, f32[6,8,256]{2,1,0:T(8,128)S(1)}, u32[]{:S(2)}, u32[]{:S(2)}) collective-permute-start(f32[6,8,256]{2,1,0:T(8,128)} %get-tuple-element.14), channel_id=1, source_target_pairs={{0,1},{1,0},{2,3},{3,2},{4,5},{5,4},{6,7},{7,6},{8,9},{9,8},{10,11... | collective-permute-start | bytes 147464 | tf_op jit(solution)/shard_map/ppermute | solution.py:352
  20.2 9.4 %collective-permute-start.3 = (f32[8,256]{1,0:T(8,128)}, f32[8,256]{1,0:T(8,128)S(1)}, u32[]{:S(2)}, u32[]{:S(2)}) collective-permute-start(f32[8,256]{1,0:T(8,128)} %get-tuple-element.15), channel_id=1, source_target_pairs={{0,3},{1,2},{2,5},{3,4},{4,7},{5,6},{6,9},{7,8},{8,11},{9,10},{10,... | collective-permute-start | bytes 24584 | tf_op jit(solution)/shard_map/ppermute | solution.py:351
  22.2 1.1 %copy-start.3 = (f32[3,4,64,256]{3,2,1,0:T(8,128)S(1)}, f32[3,4,64,256]{3,2,1,0:T(8,128)}, u32[]{:S(2)}) copy-start(f32[3,4,64,256]{3,2,1,0:T(8,128)} %refs_0_.3) | copy-start | bytes 2359300
  25.5 11.4 %copy-start.6 = (s32[4]{0:T(128)S(1)}, s32[4]{0:T(128)}, u32[]{:S(2)}) copy-start(s32[4]{0:T(128)} %bits.1) | copy-start | bytes 52
  25.5 11.6 %copy-start.7 = (s32[256,4]{0,1:T(4,128)S(1)}, s32[256,4]{0,1:T(4,128)}, u32[]{:S(2)}) copy-start(s32[256,4]{0,1:T(4,128)} %param.10) | copy-start | bytes 12292
  31.5 6.7 %copy-start.8 = (f32[8,256]{1,0:T(8,128)S(1)}, f32[8,256]{1,0:T(8,128)}, u32[]{:S(2)}) copy-start(f32[8,256]{1,0:T(8,128)} %get-tuple-element.17) | copy-start | bytes 24580
  31.5 29.8 %all-to-all-start = ((f32[16,48,128]{2,1,0:T(8,128)}), f32[16,48,128]{2,1,0:T(8,128)}, u32[]{:S(2)}, u32[]{:S(2)}) async-start(f32[16,48,128]{2,1,0:T(8,128)} %force_below.1), calls=%async_computation | async-start | bytes 786432 | tf_op jit(solution)/shard_map/all_to_all | solution.py:312
  37.2 31.9 %copy-start.4 = (f32[3,4,64,256]{3,2,1,0:T(8,128)S(1)}, f32[3,4,64,256]{3,2,1,0:T(8,128)}, u32[]{:S(2)}) copy-start(f32[3,4,64,256]{3,2,1,0:T(8,128)} %refs_0_.3) | copy-start | bytes 2359300
  38.1 14.3 %collective-permute-start.4 = (f32[8,256]{1,0:T(8,128)S(1)}, f32[8,256]{1,0:T(8,128)S(1)}, u32[]{:S(2)}, u32[]{:S(2)}) collective-permute-start(f32[8,256]{1,0:T(8,128)S(1)} %copy-done.8), channel_id=1, source_target_pairs={{2,1},{3,0},{4,3},{5,2},{6,5},{7,4},{8,7},{9,6},{10,9},{11,8},{12,... | collective-permute-start | bytes 24584 | tf_op jit(solution)/shard_map/ppermute | solution.py:387
  62.5 0.7 copy-start.5
  63.2 30.2 %all-to-all-start.1 = ((f32[16,48,128]{2,1,0:T(8,128)}), f32[16,48,128]{2,1,0:T(8,128)}, u32[]{:S(2)}, u32[]{:S(2)}) async-start(f32[16,48,128]{2,1,0:T(8,128)} %copy-done.5), calls=%async_computation.1 | async-start | bytes 786432 | tf_op jit(solution)/shard_map/all_to_all | solution.py:312

commit v4 on v3

--- a/solution.py
+++ b/solution.py
@@ -404,9 +404,9 @@
     return pl.pallas_call(
         place_kernel,
         out_shape=shape((6, planes, rows, cells), f32),
-        in_specs=[anywhere, pl.BlockSpec(group_shape, lambda i: (0, 0, 0))],
-        out_specs=pl.BlockSpec((6, 1, rows, cells), lambda i: (0, 0, 0, 0)),
-        grid=(1,),
+        in_specs=[anywhere, pl.BlockSpec((GROUP // 4, 48, LANES), lambda i: (i, 0, 0))],
+        out_specs=pl.BlockSpec((6, 1, rows // 4, cells), lambda i: (0, 0, i, 0)),
+        grid=(4,),
         input_output_aliases={0: 0},
         compiler_params=PARAMS,
         name="place",

time: 95.9 us -> 97.2 us (1.014)
  Pallas kernels: 17.3 us -> 18.6 us
    pallas_call x1, Pallas kernels: 1.84 us -> 3.13 us  [on_device(): pl.pallas_call(place_kernel, out_shape=shape((6, planes, rows, cells), f3...]
where the time goes in v4:
time: 97.2 us; the launch traced here: 96.6 us
  starting transfers between devices  37.4 us (38%)
  waiting for transfers between devices  37.2 us (38%)
  Pallas kernels  18.6 us (19%)
  local copies, waits for them, and re-layouts  3.11 us (3%)
    all_to_all x2, waiting for transfers between devices, exchange(): return lax.all_to_all(block, 'slab', 0, 0, axis_index_groups=groups)  25.6 us
    ppermute x1, starting transfers between devices, on_device(): down = lax.ppermute(down, 'slab', downward)  11.9 us
    pallas_call x3, Pallas kernels, forces(): pl.pallas_call(functools.partial(force_kernel, targets, low, high, tuple(...  11.8 us
    all_to_all x2, starting transfers between devices, exchange(): return lax.all_to_all(block, 'slab', 0, 0, axis_index_groups=groups)  11.3 us
    ppermute x1, waiting for transfers between devices, on_device(): edge_down = lax.ppermute(edge_down, both, across_down)  7.53 us
    ppermute x1, starting transfers between devices, on_device(): edge_down = lax.ppermute(edge_down, both, across_down)  6.55 us
    ppermute x1, waiting for transfers between devices, on_device(): edge_up = lax.ppermute(edge_up, both, across_up)  4.05 us
    ppermute x1, starting transfers between devices, on_device(): up = lax.ppermute(up, 'slab', upward)  3.83 us
  transfers between devices with their start and end apart: 7, of which 4 were waited for; matrix products, arithmetic and copies ran while one was open for 1% of the time, Pallas kernels for 10%

profile of v4, /device:TPU:24, one launch (start us, length us, event | category | flops | bytes accessed | tf_op | source)
XLA Modules:
  0.0 96.6 jit_solution(12085472516309389525)
XLA Ops:
  0.0 2.5 %pack.1 = (f32[8,64,256]{2,1,0:T(8,128)}, f32[6,64,256]{2,1,0:T(8,128)}, f32[6,8,256]{2,1,0:T(8,128)}, f32[8,256]{1,0:T(8,128)}, f32[8,256]{1,0:T(8,128)}) custom-call(f32[3,4,64,256]{3,2,1,0:T(8,128)} %refs_7_.1, f32[4,64,256]{2,1,0:T(8,128)} %refs_8_.1, s32[2,4,64,256]{3,2,1,0:T(8,128)} %refs_1_.3), custom_call_target="tpu_custom_call" | custom-call | tf_op jit(solution)/shard_map/pack/pallas_call | solution.py:328
  2.5 3.8 %collective-permute-start = (f32[8,64,256]{2,1,0:T(8,128)}, f32[8,64,256]{2,1,0:T(8,128)S(1)}, u32[]{:S(2)}, u32[]{:S(2)}) collective-permute-start(f32[8,64,256]{2,1,0:T(8,128)} %get-tuple-element.12), channel_id=1, source_target_pairs={{0,2},{2,4},{4,6},{6,8},{8,10},{10,12},{12,14},{14,16},{16,18},{18... | collective-permute-start | bytes 1572872 | tf_op jit(solution)/shard_map/ppermute | solution.py:350
  6.4 11.9 %collective-permute-start.1 = (f32[6,64,256]{2,1,0:T(8,128)}, f32[6,64,256]{2,1,0:T(8,128)S(1)}, u32[]{:S(2)}, u32[]{:S(2)}) collective-permute-start(f32[6,64,256]{2,1,0:T(8,128)} %get-tuple-element.13), channel_id=1, source_target_pairs={{2,0},{4,2},{6,4},{8,6},{10,8},{12,10},{14,12},{16,14},{18,16},{20... | collective-permute-start | bytes 1179656 | tf_op jit(solution)/shard_map/ppermute | solution.py:353
  18.3 1.9 %collective-permute-start.2 = (f32[6,8,256]{2,1,0:T(8,128)}, f32[6,8,256]{2,1,0:T(8,128)S(1)}, u32[]{:S(2)}, u32[]{:S(2)}) collective-permute-start(f32[6,8,256]{2,1,0:T(8,128)} %get-tuple-element.14), channel_id=1, source_target_pairs={{0,1},{1,0},{2,3},{3,2},{4,5},{5,4},{6,7},{7,6},{8,9},{9,8},{10,11... | collective-permute-start | bytes 147464 | tf_op jit(solution)/shard_map/ppermute | solution.py:352
  20.2 1.9 %collective-permute-start.3 = (f32[8,256]{1,0:T(8,128)}, f32[8,256]{1,0:T(8,128)S(1)}, u32[]{:S(2)}, u32[]{:S(2)}) collective-permute-start(f32[8,256]{1,0:T(8,128)} %get-tuple-element.15), channel_id=1, source_target_pairs={{0,3},{1,2},{2,5},{3,4},{4,7},{5,6},{6,9},{7,8},{8,11},{9,10},{10,... | collective-permute-start | bytes 24584 | tf_op jit(solution)/shard_map/ppermute | solution.py:351
  22.1 0.0 collective-permute-done.2.refs_2_.refs_4_
  22.2 0.0 copy-start.3
  22.2 1.1 %copy-done.3 = f32[3,4,64,256]{3,2,1,0:T(8,128)S(1)} copy-done((f32[3,4,64,256]{3,2,1,0:T(8,128)S(1)}, f32[3,4,64,256]{3,2,1,0:T(8,128)}, u32[]{:S(2)}) %copy-start.3) | copy-done | bytes 786456
  23.3 2.2 %force_own.1.refs_0_ = f32[3,1,64,256]{3,2,1,0:T(8,128)S(1)} custom-call(f32[3,4,64,256]{3,2,1,0:T(8,128)S(1)} %copy-done.3, s32[2,4,64,256]{3,2,1,0:T(8,128)S(1)} %copy-done.1, f32[6,8,256]{2,1,0:T(8,128)S(1)} %collective-permute-done.2.refs_2_.refs_4_, f32[3,4,64,256]{3,2,1,0:T(8,128)S(1)} %copy-done, f32[4,64,256]{2,1,0:T(8,128)S(1)} %copy-done.2), custom_call_target="tpu_custom_call" | custom-call | tf_op jit(solution)/shard_map/force_own/pallas_call | solution.py:363
  25.5 0.0 copy-start.6
  25.5 0.0 copy-start.7
  25.5 4.1 %collective-permute-done.3.refs_2_.refs_5_ = f32[8,256]{1,0:T(8,128)S(1)} collective-permute-done((f32[8,256]{1,0:T(8,128)}, f32[8,256]{1,0:T(8,128)S(1)}, u32[]{:S(2)}, u32[]{:S(2)}) %collective-permute-start.3) | collective-permute-done | bytes 8224 | tf_op jit(solution)/shard_map/ppermute | solution.py:351
  29.6 0.0 collective-permute-done.1.refs_3_
  29.6 0.0 collective-permute-done.refs_1_.refs_2_
  29.6 1.9 %force_below.1 = f32[16,48,128]{2,1,0:T(8,128)} custom-call(f32[3,1,64,256]{3,2,1,0:T(8,128)S(1)} %force_own.1.refs_0_, f32[8,64,256]{2,1,0:T(8,128)S(1)} %collective-permute-done.refs_1_.refs_2_, f32[8,256]{1,0:T(8,128)S(1)} %collective-permute-done.3.refs_2_.refs_5_, f32[6,64,256]{2,1,0:T(8,128)S(1)} %collective-permute-done.1.refs_3_, ...), custom_call_target="tpu_custom_call" | custom-call | tf_op jit(solution)/shard_map/force_below/pallas_call | solution.py:363
  31.5 5.4 %all-to-all-start = ((f32[16,48,128]{2,1,0:T(8,128)}), f32[16,48,128]{2,1,0:T(8,128)}, u32[]{:S(2)}, u32[]{:S(2)}) async-start(f32[16,48,128]{2,1,0:T(8,128)} %force_below.1), calls=%async_computation | async-start | bytes 786432 | tf_op jit(solution)/shard_map/all_to_all | solution.py:312
  36.9 0.1 fusion.2
  37.0 0.1 reshape.62
  37.1 0.1 dynamic-slice_bitcast_fusion
  37.2 0.9 gather_fusion
  38.1 0.1 reshape.65
  38.1 6.5 %collective-permute-start.4 = (f32[8,256]{1,0:T(8,128)S(1)}, f32[8,256]{1,0:T(8,128)S(1)}, u32[]{:S(2)}, u32[]{:S(2)}) collective-permute-start(f32[8,256]{1,0:T(8,128)S(1)} %copy-done.8), channel_id=1, source_target_pairs={{2,1},{3,0},{4,3},{5,2},{6,5},{7,4},{8,7},{9,6},{10,9},{11,8},{12,... | collective-permute-start | bytes 24584 | tf_op jit(solution)/shard_map/ppermute | solution.py:387
  44.7 0.1 select_minimum_fusion
  44.8 0.1 reshape.61.taken
  44.9 7.5 %collective-permute-done.4.refs_6_.order = f32[8,256]{1,0:T(8,128)S(1)} collective-permute-done((f32[8,256]{1,0:T(8,128)S(1)}, f32[8,256]{1,0:T(8,128)S(1)}, u32[]{:S(2)}, u32[]{:S(2)}) %collective-permute-start.4) | collective-permute-done | bytes 8224 | tf_op jit(solution)/shard_map/ppermute | solution.py:387
  52.4 8.9 %all-to-all-done.data = f32[16,48,128]{2,1,0:T(8,128)} async-done(((f32[16,48,128]{2,1,0:T(8,128)}), f32[16,48,128]{2,1,0:T(8,128)}, u32[]{:S(2)}, u32[]{:S(2)}) %all-to-all-start) | async-done | bytes 393248 | tf_op jit(solution)/shard_map/all_to_all | solution.py:312
  61.3 1.2 %route.1 = f32[16,48,128]{2,1,0:T(8,128)S(1)} custom-call(s32[64]{0:T(128)S(1)} %reshape.61.taken, s32[4]{0:T(128)S(1)} %copy-done.6, f32[16,48,128]{2,1,0:T(8,128)} %all-to-all-done.data, f32[8,256]{1,0:T(8,128)S(1)} %collective-permute-done.4.refs_6_.order), custom_call_target="tpu_custom_call" | custom-call | tf_op jit(solution)/shard_map/route/pallas_call | solution.py:394
  62.5 0.7 copy-done.5
  63.2 5.9 %all-to-all-start.1 = ((f32[16,48,128]{2,1,0:T(8,128)}), f32[16,48,128]{2,1,0:T(8,128)}, u32[]{:S(2)}, u32[]{:S(2)}) async-start(f32[16,48,128]{2,1,0:T(8,128)} %copy-done.5), calls=%async_computation.1 | async-start | bytes 786432 | tf_op jit(solution)/shard_map/all_to_all | solution.py:312
  69.1 7.6 %force_rest.1.whole = f32[6,4,64,256]{3,2,1,0:T(8,128)} custom-call(f32[3,4,64,256]{3,2,1,0:T(8,128)S(1)} %copy-done.4, s32[2,4,64,256]{3,2,1,0:T(8,128)S(1)} %copy-done.1, f32[8,64,256]{2,1,0:T(8,128)S(1)} %collective-permute-done.refs_1_.refs_2_, f32[6,64,256]{2,1,0:T(8,128)S(1)} %collective-permute-done.1.refs_3_, ...), custom_call_target="tpu_custom_call" | custom-call | tf_op jit(solution)/shard_map/force_rest/pallas_call | solution.py:363
  76.8 16.7 %all-to-all-done.1.columns = f32[16,48,128]{2,1,0:T(8,128)} async-done(((f32[16,48,128]{2,1,0:T(8,128)}), f32[16,48,128]{2,1,0:T(8,128)}, u32[]{:S(2)}, u32[]{:S(2)}) %all-to-all-start.1) | async-done | bytes 393248 | tf_op jit(solution)/shard_map/all_to_all | solution.py:312
  93.5 3.1 %place.1 = f32[6,4,64,256]{3,2,1,0:T(8,128)} custom-call(f32[6,4,64,256]{3,2,1,0:T(8,128)} %force_rest.1.whole, f32[16,48,128]{2,1,0:T(8,128)} %all-to-all-done.1.columns), custom_call_target="tpu_custom_call", output_to_operand_aliasing={{}: (0, {})} | custom-call | tf_op jit(solution)/shard_map/place/pallas_call | solution.py:404
  (14 shorter events, 0.0 us)
Async XLA Ops:
  0.0 22.1 %copy-start.2 = (f32[4,64,256]{2,1,0:T(8,128)S(1)}, f32[4,64,256]{2,1,0:T(8,128)}, u32[]{:S(2)}) copy-start(f32[4,64,256]{2,1,0:T(8,128)} %refs_8_.1) | copy-start | bytes 786436
  0.0 22.1 %copy-start = (f32[3,4,64,256]{3,2,1,0:T(8,128)S(1)}, f32[3,4,64,256]{3,2,1,0:T(8,128)}, u32[]{:S(2)}) copy-start(f32[3,4,64,256]{3,2,1,0:T(8,128)} %refs_7_.1) | copy-start | bytes 2359300
  0.0 22.1 %copy-start.1 = (s32[2,4,64,256]{3,2,1,0:T(8,128)S(1)}, s32[2,4,64,256]{3,2,1,0:T(8,128)}, u32[]{:S(2)}) copy-start(s32[2,4,64,256]{3,2,1,0:T(8,128)} %refs_1_.3) | copy-start | bytes 1572868
  2.5 27.0 %collective-permute-start = (f32[8,64,256]{2,1,0:T(8,128)}, f32[8,64,256]{2,1,0:T(8,128)S(1)}, u32[]{:S(2)}, u32[]{:S(2)}) collective-permute-start(f32[8,64,256]{2,1,0:T(8,128)} %get-tuple-element.12), channel_id=1, source_target_pairs={{0,2},{2,4},{4,6},{6,8},{8,10},{10,12},{12,14},{14,16},{16,18},{18... | collective-permute-start | bytes 1572872 | tf_op jit(solution)/shard_map/ppermute | solution.py:350
  6.4 23.2 %collective-permute-start.1 = (f32[6,64,256]{2,1,0:T(8,128)}, f32[6,64,256]{2,1,0:T(8,128)S(1)}, u32[]{:S(2)}, u32[]{:S(2)}) collective-permute-start(f32[6,64,256]{2,1,0:T(8,128)} %get-tuple-element.13), channel_id=1, source_target_pairs={{2,0},{4,2},{6,4},{8,6},{10,8},{12,10},{14,12},{16,14},{18,16},{20... | collective-permute-start | bytes 1179656 | tf_op jit(solution)/shard_map/ppermute | solution.py:353
  18.3 3.9 %collective-permute-start.2 = (f32[6,8,256]{2,1,0:T(8,128)}, f32[6,8,256]{2,1,0:T(8,128)S(1)}, u32[]{:S(2)}, u32[]{:S(2)}) collective-permute-start(f32[6,8,256]{2,1,0:T(8,128)} %get-tuple-element.14), channel_id=1, source_target_pairs={{0,1},{1,0},{2,3},{3,2},{4,5},{5,4},{6,7},{7,6},{8,9},{9,8},{10,11... | collective-permute-start | bytes 147464 | tf_op jit(solution)/shard_map/ppermute | solution.py:352
  20.2 9.4 %collective-permute-start.3 = (f32[8,256]{1,0:T(8,128)}, f32[8,256]{1,0:T(8,128)S(1)}, u32[]{:S(2)}, u32[]{:S(2)}) collective-permute-start(f32[8,256]{1,0:T(8,128)} %get-tuple-element.15), channel_id=1, source_target_pairs={{0,3},{1,2},{2,5},{3,4},{4,7},{5,6},{6,9},{7,8},{8,11},{9,10},{10,... | collective-permute-start | bytes 24584 | tf_op jit(solution)/shard_map/ppermute | solution.py:351
  22.2 1.1 %copy-start.3 = (f32[3,4,64,256]{3,2,1,0:T(8,128)S(1)}, f32[3,4,64,256]{3,2,1,0:T(8,128)}, u32[]{:S(2)}) copy-start(f32[3,4,64,256]{3,2,1,0:T(8,128)} %refs_0_.3) | copy-start | bytes 2359300
  25.5 11.4 %copy-start.6 = (s32[4]{0:T(128)S(1)}, s32[4]{0:T(128)}, u32[]{:S(2)}) copy-start(s32[4]{0:T(128)} %bits.1) | copy-start | bytes 52
  25.5 11.6 %copy-start.7 = (s32[256,4]{0,1:T(4,128)S(1)}, s32[256,4]{0,1:T(4,128)}, u32[]{:S(2)}) copy-start(s32[256,4]{0,1:T(4,128)} %param.10) | copy-start | bytes 12292
  31.5 6.7 %copy-start.8 = (f32[8,256]{1,0:T(8,128)S(1)}, f32[8,256]{1,0:T(8,128)}, u32[]{:S(2)}) copy-start(f32[8,256]{1,0:T(8,128)} %get-tuple-element.17) | copy-start | bytes 24580
  31.5 29.8 %all-to-all-start = ((f32[16,48,128]{2,1,0:T(8,128)}), f32[16,48,128]{2,1,0:T(8,128)}, u32[]{:S(2)}, u32[]{:S(2)}) async-start(f32[16,48,128]{2,1,0:T(8,128)} %force_below.1), calls=%async_computation | async-start | bytes 786432 | tf_op jit(solution)/shard_map/all_to_all | solution.py:312
  37.2 31.9 %copy-start.4 = (f32[3,4,64,256]{3,2,1,0:T(8,128)S(1)}, f32[3,4,64,256]{3,2,1,0:T(8,128)}, u32[]{:S(2)}) copy-start(f32[3,4,64,256]{3,2,1,0:T(8,128)} %refs_0_.3) | copy-start | bytes 2359300
  38.1 14.3 %collective-permute-start.4 = (f32[8,256]{1,0:T(8,128)S(1)}, f32[8,256]{1,0:T(8,128)S(1)}, u32[]{:S(2)}, u32[]{:S(2)}) collective-permute-start(f32[8,256]{1,0:T(8,128)S(1)} %copy-done.8), channel_id=1, source_target_pairs={{2,1},{3,0},{4,3},{5,2},{6,5},{7,4},{8,7},{9,6},{10,9},{11,8},{12,... | collective-permute-start | bytes 24584 | tf_op jit(solution)/shard_map/ppermute | solution.py:387
  62.5 0.7 copy-start.5
  63.2 30.2 %all-to-all-start.1 = ((f32[16,48,128]{2,1,0:T(8,128)}), f32[16,48,128]{2,1,0:T(8,128)}, u32[]{:S(2)}, u32[]{:S(2)}) async-start(f32[16,48,128]{2,1,0:T(8,128)} %copy-done.5), calls=%async_computation.1 | async-start | bytes 786432 | tf_op jit(solution)/shard_map/all_to_all | solution.py:312

commit v5 on v3

--- a/solution.py
+++ b/solution.py
@@ -269,17 +269,23 @@
     lax.fori_loop(0, rows // 8, block, 0)
 
 
-def route_kernel(taken, bits, data, order, out, scratch):
+def route_kernel(taken, bits, data, order, out, scratch, sems):
     del order
     member = lax.rem(lax.axis_index("slab"), GROUP)
     column = 4 * member + lax.rem(lax.broadcasted_iota(jnp.int32, (48, LANES), 0), 4)
+    copies = []
     for turn in range(4):
         source = data if turn == 0 else scratch.at[(turn - 1) % 2]
-        target = out if turn == 3 else scratch.at[turn % 2]
+        target = scratch.at[turn % 2]
         distance = jnp.left_shift(jnp.int32(1), bits[turn])
         for slab in range(GROUP):
             moved = column < taken[turn * GROUP + slab]
             target[slab] = jnp.where(moved, source[jnp.bitwise_xor(slab, distance)], source[slab])
+            if turn == 3:
+                copies.append(pltpu.make_async_copy(target.at[slab], out.at[slab], sems.at[slab]))
+                copies[-1].start()
+    for copy in copies:
+        copy.wait()
 
 
 def place_kernel(whole, columns, out):
@@ -395,9 +401,9 @@
         route_kernel,
         out_shape=shape(group_shape, f32),
         in_specs=[SMEM, SMEM, VMEM, anywhere],
-        out_specs=VMEM,
-        scratch_shapes=[pltpu.VMEM((2,) + group_shape, f32)],
-        compiler_params=PARAMS,
+        out_specs=anywhere,
+        scratch_shapes=[pltpu.VMEM((2,) + group_shape, f32), pltpu.SemaphoreType.DMA((GROUP,))],
+        compiler_params=ALONE,
         name="route",
     )(taken, bits, columns, edge_down)
     columns = exchange(columns)

time: 95.9 us -> 96.9 us (1.010)
  transfers between devices with their start and end apart: 7 -> 7, of which waited for: 4 -> 4; matrix products, arithmetic and copies ran while one was open for 1% -> 2% of each run, Pallas kernels for 10% -> 10%
where the time goes in v5:
time: 96.9 us; the launch traced here: 96.3 us
  starting transfers between devices  37.8 us (39%)
  waiting for transfers between devices  36.3 us (37%)
  Pallas kernels  18.2 us (19%)
  local copies, waits for them, and re-layouts  3.64 us (4%)
    all_to_all x2, waiting for transfers between devices, exchange(): return lax.all_to_all(block, 'slab', 0, 0, axis_index_groups=groups)  25.3 us
    ppermute x1, starting transfers between devices, on_device(): down = lax.ppermute(down, 'slab', downward)  11.9 us
    pallas_call x3, Pallas kernels, forces(): pl.pallas_call(functools.partial(force_kernel, targets, low, high, tuple(...  11.8 us
    all_to_all x2, starting transfers between devices, exchange(): return lax.all_to_all(block, 'slab', 0, 0, axis_index_groups=groups)  11.7 us
    ppermute x1, waiting for transfers between devices, on_device(): edge_down = lax.ppermute(edge_down, both, across_down)  6.95 us
    ppermute x1, starting transfers between devices, on_device(): edge_down = lax.ppermute(edge_down, both, across_down)  6.55 us
    ppermute x1, waiting for transfers between devices, on_device(): edge_up = lax.ppermute(edge_up, both, across_up)  4.05 us
    ppermute x1, starting transfers between devices, on_device(): up = lax.ppermute(up, 'slab', upward)  3.83 us
  transfers between devices with their start and end apart: 7, of which 4 were waited for; matrix products, arithmetic and copies ran while one was open for 2% of the time, Pallas kernels for 10%

profile of v5, /device:TPU:24, one launch (start us, length us, event | category | flops | bytes accessed | tf_op | source)
XLA Modules:
  0.0 96.3 jit_solution(238879193644825803)
XLA Ops:
  0.0 2.5 %pack.1 = (f32[8,64,256]{2,1,0:T(8,128)}, f32[6,64,256]{2,1,0:T(8,128)}, f32[6,8,256]{2,1,0:T(8,128)}, f32[8,256]{1,0:T(8,128)}, f32[8,256]{1,0:T(8,128)}) custom-call(f32[3,4,64,256]{3,2,1,0:T(8,128)} %refs_7_.1, f32[4,64,256]{2,1,0:T(8,128)} %refs_8_.1, s32[2,4,64,256]{3,2,1,0:T(8,128)} %refs_1_.3), custom_call_target="tpu_custom_call" | custom-call | tf_op jit(solution)/shard_map/pack/pallas_call | solution.py:334
  2.5 3.8 %collective-permute-start = (f32[8,64,256]{2,1,0:T(8,128)}, f32[8,64,256]{2,1,0:T(8,128)S(1)}, u32[]{:S(2)}, u32[]{:S(2)}) collective-permute-start(f32[8,64,256]{2,1,0:T(8,128)} %get-tuple-element.12), channel_id=1, source_target_pairs={{0,2},{2,4},{4,6},{6,8},{8,10},{10,12},{12,14},{14,16},{16,18},{18... | collective-permute-start | bytes 1572872 | tf_op jit(solution)/shard_map/ppermute | solution.py:356
  6.4 11.9 %collective-permute-start.1 = (f32[6,64,256]{2,1,0:T(8,128)}, f32[6,64,256]{2,1,0:T(8,128)S(1)}, u32[]{:S(2)}, u32[]{:S(2)}) collective-permute-start(f32[6,64,256]{2,1,0:T(8,128)} %get-tuple-element.13), channel_id=1, source_target_pairs={{2,0},{4,2},{6,4},{8,6},{10,8},{12,10},{14,12},{16,14},{18,16},{20... | collective-permute-start | bytes 1179656 | tf_op jit(solution)/shard_map/ppermute | solution.py:359
  18.3 1.9 %collective-permute-start.2 = (f32[6,8,256]{2,1,0:T(8,128)}, f32[6,8,256]{2,1,0:T(8,128)S(1)}, u32[]{:S(2)}, u32[]{:S(2)}) collective-permute-start(f32[6,8,256]{2,1,0:T(8,128)} %get-tuple-element.14), channel_id=1, source_target_pairs={{0,1},{1,0},{2,3},{3,2},{4,5},{5,4},{6,7},{7,6},{8,9},{9,8},{10,11... | collective-permute-start | bytes 147464 | tf_op jit(solution)/shard_map/ppermute | solution.py:358
  20.2 1.9 %collective-permute-start.3 = (f32[8,256]{1,0:T(8,128)}, f32[8,256]{1,0:T(8,128)S(1)}, u32[]{:S(2)}, u32[]{:S(2)}) collective-permute-start(f32[8,256]{1,0:T(8,128)} %get-tuple-element.15), channel_id=1, source_target_pairs={{0,3},{1,2},{2,5},{3,4},{4,7},{5,6},{6,9},{7,8},{8,11},{9,10},{10,... | collective-permute-start | bytes 24584 | tf_op jit(solution)/shard_map/ppermute | solution.py:357
  22.1 0.0 collective-permute-done.2.refs_2_.refs_4_
  22.2 0.0 copy-start.3
  22.2 1.1 %copy-done.3 = f32[3,4,64,256]{3,2,1,0:T(8,128)S(1)} copy-done((f32[3,4,64,256]{3,2,1,0:T(8,128)S(1)}, f32[3,4,64,256]{3,2,1,0:T(8,128)}, u32[]{:S(2)}) %copy-start.3) | copy-done | bytes 786456
  23.3 2.2 %force_own.1.refs_0_ = f32[3,1,64,256]{3,2,1,0:T(8,128)S(1)} custom-call(f32[3,4,64,256]{3,2,1,0:T(8,128)S(1)} %copy-done.3, s32[2,4,64,256]{3,2,1,0:T(8,128)S(1)} %copy-done.1, f32[6,8,256]{2,1,0:T(8,128)S(1)} %collective-permute-done.2.refs_2_.refs_4_, f32[3,4,64,256]{3,2,1,0:T(8,128)S(1)} %copy-done, f32[4,64,256]{2,1,0:T(8,128)S(1)} %copy-done.2), custom_call_target="tpu_custom_call" | custom-call | tf_op jit(solution)/shard_map/force_own/pallas_call | solution.py:369
  25.5 0.0 copy-start.8
  25.5 0.0 copy-start.7
  25.5 4.1 %collective-permute-done.3.refs_2_.refs_5_ = f32[8,256]{1,0:T(8,128)S(1)} collective-permute-done((f32[8,256]{1,0:T(8,128)}, f32[8,256]{1,0:T(8,128)S(1)}, u32[]{:S(2)}, u32[]{:S(2)}) %collective-permute-start.3) | collective-permute-done | bytes 8224 | tf_op jit(solution)/shard_map/ppermute | solution.py:357
  29.6 0.0 collective-permute-done.1.refs_3_
  29.6 0.0 collective-permute-done.refs_1_.refs_2_
  29.6 1.9 %force_below.1 = f32[16,48,128]{2,1,0:T(8,128)} custom-call(f32[3,1,64,256]{3,2,1,0:T(8,128)S(1)} %force_own.1.refs_0_, f32[8,64,256]{2,1,0:T(8,128)S(1)} %collective-permute-done.refs_1_.refs_2_, f32[8,256]{1,0:T(8,128)S(1)} %collective-permute-done.3.refs_2_.refs_5_, f32[6,64,256]{2,1,0:T(8,128)S(1)} %collective-permute-done.1.refs_3_, ...), custom_call_target="tpu_custom_call" | custom-call | tf_op jit(solution)/shard_map/force_below/pallas_call | solution.py:369
  31.5 5.4 %all-to-all-start = ((f32[16,48,128]{2,1,0:T(8,128)}), f32[16,48,128]{2,1,0:T(8,128)}, u32[]{:S(2)}, u32[]{:S(2)}) async-start(f32[16,48,128]{2,1,0:T(8,128)} %force_below.1), calls=%async_computation | async-start | bytes 786432 | tf_op jit(solution)/shard_map/all_to_all | solution.py:318
  36.9 0.1 fusion.2
  37.0 0.1 reshape.62
  37.1 0.1 dynamic-slice_bitcast_fusion
  37.2 0.9 gather_fusion
  38.1 0.1 reshape.65
  38.1 6.5 %collective-permute-start.4 = (f32[8,256]{1,0:T(8,128)S(1)}, f32[8,256]{1,0:T(8,128)S(1)}, u32[]{:S(2)}, u32[]{:S(2)}) collective-permute-start(f32[8,256]{1,0:T(8,128)S(1)} %copy-done.9), channel_id=1, source_target_pairs={{2,1},{3,0},{4,3},{5,2},{6,5},{7,4},{8,7},{9,6},{10,9},{11,8},{12,... | collective-permute-start | bytes 24584 | tf_op jit(solution)/shard_map/ppermute | solution.py:393
  44.7 0.1 select_minimum_fusion
  44.8 0.7 reshape.61.taken
  45.5 7.0 %collective-permute-done.4.refs_6_.order = f32[8,256]{1,0:T(8,128)S(1)} collective-permute-done((f32[8,256]{1,0:T(8,128)S(1)}, f32[8,256]{1,0:T(8,128)S(1)}, u32[]{:S(2)}, u32[]{:S(2)}) %collective-permute-start.4) | collective-permute-done | bytes 8224 | tf_op jit(solution)/shard_map/ppermute | solution.py:393
  52.4 8.9 %all-to-all-done.data = f32[16,48,128]{2,1,0:T(8,128)} async-done(((f32[16,48,128]{2,1,0:T(8,128)}), f32[16,48,128]{2,1,0:T(8,128)}, u32[]{:S(2)}, u32[]{:S(2)}) %all-to-all-start) | async-done | bytes 393248 | tf_op jit(solution)/shard_map/all_to_all | solution.py:318
  61.3 2.0 %route.1 = f32[16,48,128]{2,1,0:T(8,128)} custom-call(s32[64]{0:T(128)} %reshape.61.taken, s32[4]{0:T(128)} %bits.1, f32[16,48,128]{2,1,0:T(8,128)} %all-to-all-done.data, f32[8,256]{1,0:T(8,128)} %copy-done.5), custom_call_target="tpu_custom_call" | custom-call | tf_op jit(solution)/shard_map/route/pallas_call | solution.py:400
  63.3 6.3 %all-to-all-start.1 = ((f32[16,48,128]{2,1,0:T(8,128)}), f32[16,48,128]{2,1,0:T(8,128)}, u32[]{:S(2)}, u32[]{:S(2)}) async-start(f32[16,48,128]{2,1,0:T(8,128)} %route.1), calls=%async_computation.1 | async-start | bytes 786432 | tf_op jit(solution)/shard_map/all_to_all | solution.py:318
  69.7 0.7 copy-done.6
  70.4 7.6 %force_rest.1.whole = f32[6,4,64,256]{3,2,1,0:T(8,128)} custom-call(f32[3,4,64,256]{3,2,1,0:T(8,128)S(1)} %copy-done.4, s32[2,4,64,256]{3,2,1,0:T(8,128)S(1)} %copy-done.1, f32[8,64,256]{2,1,0:T(8,128)S(1)} %collective-permute-done.refs_1_.refs_2_, f32[6,64,256]{2,1,0:T(8,128)S(1)} %collective-permute-done.1.refs_3_, ...), custom_call_target="tpu_custom_call" | custom-call | tf_op jit(solution)/shard_map/force_rest/pallas_call | solution.py:369
  78.0 16.4 %all-to-all-done.1.columns = f32[16,48,128]{2,1,0:T(8,128)} async-done(((f32[16,48,128]{2,1,0:T(8,128)}), f32[16,48,128]{2,1,0:T(8,128)}, u32[]{:S(2)}, u32[]{:S(2)}) %all-to-all-start.1) | async-done | bytes 393248 | tf_op jit(solution)/shard_map/all_to_all | solution.py:318
  94.4 1.8 %place.1 = f32[6,4,64,256]{3,2,1,0:T(8,128)} custom-call(f32[6,4,64,256]{3,2,1,0:T(8,128)} %force_rest.1.whole, f32[16,48,128]{2,1,0:T(8,128)} %all-to-all-done.1.columns), custom_call_target="tpu_custom_call", output_to_operand_aliasing={{}: (0, {})} | custom-call | tf_op jit(solution)/shard_map/place/pallas_call | solution.py:410
  (16 shorter events, 0.0 us)
Async XLA Ops:
  0.0 22.1 %copy-start.2 = (f32[4,64,256]{2,1,0:T(8,128)S(1)}, f32[4,64,256]{2,1,0:T(8,128)}, u32[]{:S(2)}) copy-start(f32[4,64,256]{2,1,0:T(8,128)} %refs_8_.1) | copy-start | bytes 786436
  0.0 22.1 %copy-start = (f32[3,4,64,256]{3,2,1,0:T(8,128)S(1)}, f32[3,4,64,256]{3,2,1,0:T(8,128)}, u32[]{:S(2)}) copy-start(f32[3,4,64,256]{3,2,1,0:T(8,128)} %refs_7_.1) | copy-start | bytes 2359300
  0.0 22.1 %copy-start.1 = (s32[2,4,64,256]{3,2,1,0:T(8,128)S(1)}, s32[2,4,64,256]{3,2,1,0:T(8,128)}, u32[]{:S(2)}) copy-start(s32[2,4,64,256]{3,2,1,0:T(8,128)} %refs_1_.3) | copy-start | bytes 1572868
  2.5 27.0 %collective-permute-start = (f32[8,64,256]{2,1,0:T(8,128)}, f32[8,64,256]{2,1,0:T(8,128)S(1)}, u32[]{:S(2)}, u32[]{:S(2)}) collective-permute-start(f32[8,64,256]{2,1,0:T(8,128)} %get-tuple-element.12), channel_id=1, source_target_pairs={{0,2},{2,4},{4,6},{6,8},{8,10},{10,12},{12,14},{14,16},{16,18},{18... | collective-permute-start | bytes 1572872 | tf_op jit(solution)/shard_map/ppermute | solution.py:356
  6.4 23.2 %collective-permute-start.1 = (f32[6,64,256]{2,1,0:T(8,128)}, f32[6,64,256]{2,1,0:T(8,128)S(1)}, u32[]{:S(2)}, u32[]{:S(2)}) collective-permute-start(f32[6,64,256]{2,1,0:T(8,128)} %get-tuple-element.13), channel_id=1, source_target_pairs={{2,0},{4,2},{6,4},{8,6},{10,8},{12,10},{14,12},{16,14},{18,16},{20... | collective-permute-start | bytes 1179656 | tf_op jit(solution)/shard_map/ppermute | solution.py:359
  18.3 3.9 %collective-permute-start.2 = (f32[6,8,256]{2,1,0:T(8,128)}, f32[6,8,256]{2,1,0:T(8,128)S(1)}, u32[]{:S(2)}, u32[]{:S(2)}) collective-permute-start(f32[6,8,256]{2,1,0:T(8,128)} %get-tuple-element.14), channel_id=1, source_target_pairs={{0,1},{1,0},{2,3},{3,2},{4,5},{5,4},{6,7},{7,6},{8,9},{9,8},{10,11... | collective-permute-start | bytes 147464 | tf_op jit(solution)/shard_map/ppermute | solution.py:358
  20.2 9.4 %collective-permute-start.3 = (f32[8,256]{1,0:T(8,128)}, f32[8,256]{1,0:T(8,128)S(1)}, u32[]{:S(2)}, u32[]{:S(2)}) collective-permute-start(f32[8,256]{1,0:T(8,128)} %get-tuple-element.15), channel_id=1, source_target_pairs={{0,3},{1,2},{2,5},{3,4},{4,7},{5,6},{6,9},{7,8},{8,11},{9,10},{10,... | collective-permute-start | bytes 24584 | tf_op jit(solution)/shard_map/ppermute | solution.py:357
  22.2 1.1 %copy-start.3 = (f32[3,4,64,256]{3,2,1,0:T(8,128)S(1)}, f32[3,4,64,256]{3,2,1,0:T(8,128)}, u32[]{:S(2)}) copy-start(f32[3,4,64,256]{3,2,1,0:T(8,128)} %refs_0_.3) | copy-start | bytes 2359300
  25.5 11.4 %copy-start.8 = (s32[4]{0:T(128)S(1)}, s32[4]{0:T(128)}, u32[]{:S(2)}) copy-start(s32[4]{0:T(128)} %bits.1) | copy-start | bytes 52
  25.5 11.6 %copy-start.7 = (s32[256,4]{0,1:T(4,128)S(1)}, s32[256,4]{0,1:T(4,128)}, u32[]{:S(2)}) copy-start(s32[256,4]{0,1:T(4,128)} %param.10) | copy-start | bytes 12292
  31.5 6.7 %copy-start.9 = (f32[8,256]{1,0:T(8,128)S(1)}, f32[8,256]{1,0:T(8,128)}, u32[]{:S(2)}) copy-start(f32[8,256]{1,0:T(8,128)} %get-tuple-element.17) | copy-start | bytes 24580
  31.5 29.8 %all-to-all-start = ((f32[16,48,128]{2,1,0:T(8,128)}), f32[16,48,128]{2,1,0:T(8,128)}, u32[]{:S(2)}, u32[]{:S(2)}) async-start(f32[16,48,128]{2,1,0:T(8,128)} %force_below.1), calls=%async_computation | async-start | bytes 786432 | tf_op jit(solution)/shard_map/all_to_all | solution.py:318
  37.2 32.5 %copy-start.4 = (f32[3,4,64,256]{3,2,1,0:T(8,128)S(1)}, f32[3,4,64,256]{3,2,1,0:T(8,128)}, u32[]{:S(2)}) copy-start(f32[3,4,64,256]{3,2,1,0:T(8,128)} %refs_0_.3) | copy-start | bytes 2359300
  38.1 14.3 %collective-permute-start.4 = (f32[8,256]{1,0:T(8,128)S(1)}, f32[8,256]{1,0:T(8,128)S(1)}, u32[]{:S(2)}, u32[]{:S(2)}) collective-permute-start(f32[8,256]{1,0:T(8,128)S(1)} %copy-done.9), channel_id=1, source_target_pairs={{2,1},{3,0},{4,3},{5,2},{6,5},{7,4},{8,7},{9,6},{10,9},{11,8},{12,... | collective-permute-start | bytes 24584 | tf_op jit(solution)/shard_map/ppermute | solution.py:393
  52.4 8.9 %copy-start.5 = (f32[8,256]{1,0:T(8,128)}, f32[8,256]{1,0:T(8,128)S(1)}, u32[]{:S(2)}) copy-start(f32[8,256]{1,0:T(8,128)S(1)} %collective-permute-done.4.refs_6_.order) | copy-start | bytes 24580
  63.3 31.1 %all-to-all-start.1 = ((f32[16,48,128]{2,1,0:T(8,128)}), f32[16,48,128]{2,1,0:T(8,128)}, u32[]{:S(2)}, u32[]{:S(2)}) async-start(f32[16,48,128]{2,1,0:T(8,128)} %route.1), calls=%async_computation.1 | async-start | bytes 786432 | tf_op jit(solution)/shard_map/all_to_all | solution.py:318
  69.7 0.7 copy-start.6
